TPU v7x, 256 devices: a whole 4x4x8 slice. The times are simulated.
256 devices in a mesh: rep: 4 (over x), node: 8 (over z), local: 8 (over y, core).
Axes of the slice: x: 4, y: 4, z: 8, core: 2. Of those that a mesh axis runs over, the one named last changes fastest.
Arguments:
- tokens: bfloat16 [32768, 3584], P(('rep', 'node', 'local')), may hold values from -6 to 6
- grad_out: bfloat16 [32768, 3584], P(('rep', 'node', 'local')), may hold values from -6 to 6
- gates: float32 [32768, 1], P(('rep', 'node', 'local')), may hold values from 0.2 to 1
- routes: int32 [32768, 1], P(('rep', 'node', 'local')), may hold values from 0 to 15; in each aligned block of 128 rows (0 to 127, 128 to 255, ...) at most 12 rows name the same one
- w_gate: bfloat16 [64, 3584, 256], P(('node', 'local')), may hold values from -0.09375 to 0.09375
- w_up: bfloat16 [64, 3584, 256], P(('node', 'local')), may hold values from -0.09375 to 0.09375
- w_down: bfloat16 [64, 256, 3584], P(('node', 'local')), may hold values from -0.1875 to 0.1875
Outputs:
- grad_tokens: bfloat16 [32768, 3584], P(('rep', 'node', 'local'))
- grad_gate: bfloat16 [64, 3584, 256], P(('node', 'local'), 'rep')
- grad_up: bfloat16 [64, 3584, 256], P(('node', 'local'), 'rep')
- grad_down: bfloat16 [64, 256, 3584], P(('node', 'local'), None, 'rep')
Inputs may be any that keep to these rules, and one draw needn't show every extreme that they name: Among the 128 tokens of one device, no expert is named by more than 12 routes; in some such block an expert is named by exactly 12.
All inputs are finite; a program needn't handle non-finite values.
Results may differ from a plain program's by a relative error of at most 0.013.
Values may be sent and summed in bfloat16 or wider, within the bound.
A program may use at most 128 MiB of HBM per device.

v0:
```python
import jax
import jax.numpy as jnp
from jax import lax
from jax.sharding import PartitionSpec as P


def on_device(tokens, grad_out, gates, routes, w_gate, w_up, w_down):
    tok_count, model_width = tokens.shape
    top_count = routes.shape[1]
    group = lax.axis_size("node") * lax.axis_size("local")
    hsplit = min(4, lax.axis_size("local"))
    experts = group // hsplit
    slots = hsplit * (
        (3 * tok_count * top_count + 2 * experts * hsplit - 1) // (2 * experts * hsplit)
    )
    piece_rows = slots // hsplit
    total_rows = tok_count * top_count
    expert_ids = routes.reshape(total_rows)
    chosen = (expert_ids[:, None] == jnp.arange(experts, dtype=jnp.int32)[None, :]).astype(
        jnp.int32
    )
    before = jnp.cumsum(chosen, axis=0) - chosen
    position = jnp.sum(before * chosen, axis=1)
    target = expert_ids * slots + position
    token_rows = tokens[:, None, :].reshape(total_rows, model_width)
    scaled = (
        (gates[:, :, None] * grad_out[:, None, :].astype(jnp.float32))
        .astype(jnp.bfloat16)
        .reshape(total_rows, model_width)
    )
    outgoing = (
        jnp.zeros((2, experts * slots, model_width), jnp.bfloat16)
        .at[:, target]
        .set(jnp.stack([token_rows, scaled]))
    )
    outgoing = outgoing.reshape(2, experts, slots, model_width)
    copies = jnp.broadcast_to(
        outgoing[:, :, None], (2, experts, hsplit, slots, model_width)
    ).reshape(2, group, slots, model_width)
    arrived = lax.all_to_all(copies, ("node", "local"), split_axis=1, concat_axis=1, tiled=True)
    arrived = arrived.reshape(2, group, hsplit, piece_rows, model_width)
    cap_rows = group * slots
    inputs = arrived[0].reshape(cap_rows, model_width)
    upstream = arrived[1].reshape(cap_rows, model_width)
    gate_block = w_gate[0]
    up_block = w_up[0]
    down_block = w_down[0]
    hidden_width = gate_block.shape[1]
    contract_last = (((1,), (1,)), ((), ()))
    contract_first = (((0,), (0,)), ((), ()))
    pre_gate = jnp.dot(inputs, gate_block, preferred_element_type=jnp.float32)
    pre_up = jnp.dot(inputs, up_block, preferred_element_type=jnp.float32)
    sigma = jax.nn.sigmoid(pre_gate)
    hidden = (pre_gate * sigma * pre_up).astype(jnp.bfloat16)
    grad_hidden = lax.dot_general(
        upstream, down_block, contract_last, preferred_element_type=jnp.float32
    )
    grad_pre_gate = (grad_hidden * pre_up * sigma * (1.0 + pre_gate * (1.0 - sigma))).astype(
        jnp.bfloat16
    )
    grad_pre_up = (grad_hidden * pre_gate * sigma).astype(jnp.bfloat16)
    both_grads = jnp.concatenate([grad_pre_gate, grad_pre_up], axis=1)
    both_weights = jnp.concatenate([gate_block, up_block], axis=1)
    partial_rows = lax.dot_general(
        both_grads, both_weights, contract_last, preferred_element_type=jnp.float32
    )
    shares = partial_rows.reshape(group, hsplit, piece_rows, model_width)
    first_term = lax.dot_general(
        inputs, both_grads, contract_first, preferred_element_type=jnp.float32
    )
    second_term = lax.dot_general(
        upstream, hidden, contract_first, preferred_element_type=jnp.float32
    )
    summed_grads = lax.psum_scatter(
        jnp.concatenate([first_term, second_term], axis=1).astype(jnp.bfloat16),
        "rep",
        scatter_dimension=0,
        tiled=True,
    ).astype(jnp.float32)
    out_gate = summed_grads[:, :hidden_width].astype(jnp.bfloat16)[None]
    out_up = summed_grads[:, hidden_width : 2 * hidden_width].astype(jnp.bfloat16)[None]
    out_down = summed_grads[:, 2 * hidden_width :].astype(jnp.bfloat16).T[None]
    returned = lax.all_to_all(
        shares.astype(jnp.bfloat16), ("node", "local"), split_axis=0, concat_axis=0, tiled=True
    ).astype(shares.dtype)
    combined = jnp.sum(returned.reshape(experts, hsplit, slots, model_width), axis=1)
    home_rows = combined.astype(jnp.bfloat16).reshape(experts * slots, model_width)
    route_grads = home_rows[target].reshape(tok_count, top_count, model_width)
    grad_tokens = jnp.sum(route_grads.astype(jnp.float32), axis=1).astype(jnp.bfloat16)
    return (grad_tokens, out_gate, out_up, out_down)


def solution(mesh):
    in_specs = (
        P(("rep", "node", "local"), None),
        P(("rep", "node", "local"), None),
        P(("rep", "node", "local"), None),
        P(("rep", "node", "local"), None),
        P(("node", "local"), None, None),
        P(("node", "local"), None, None),
        P(("node", "local"), None, None),
    )
    out_specs = (
        P(("rep", "node", "local"), None),
        P(("node", "local"), "rep", None),
        P(("node", "local"), "rep", None),
        P(("node", "local"), None, "rep"),
    )
    return jax.shard_map(
        on_device, mesh=mesh, in_specs=in_specs, out_specs=out_specs, check_vma=False
    )
```

profile of v0, /device:TPU:1, one launch (start us, length us, event | category | flops | bytes accessed | tf_op | source)
XLA Modules:
  0.0 577.2 jit_solution(1491818946748913844)
XLA Ops:
  7.2 0.9 fusion.7
  8.2 0.8 select_reduce_fusion
  9.7 1.4 fusion.5
  11.1 1.4 maximum_bitcast_fusion
  12.5 3.1 copy.20
  15.6 3.0 broadcast_in_dim.24
  18.6 17.5 %scatter_fusion = bf16[2,192,3584]{2,0,1:T(2,128)(2,1)} fusion(bf16[2,192,3584]{2,0,1:T(2,128)(2,1)} %broadcast_in_dim.24, s32[128]{0:T(128)S(1)} %fusion.8, bf16[128,2,3584]{2,1,0:T(2,128)(2,1)} %copy.20), kind=kCustom, calls=%fused_computation.1 | custom fusion | bytes 5505536 | tf_op jit(solution)/shard_map/scatter | solution.py:34
  36.1 8.4 %broadcast_in_dim.26 = bf16[2,16,4,12,3584]{4,0,3,2,1:T(2,128)(2,1)S(1)} broadcast(bf16[2,16,12,3584]{3,0,2,1:T(2,128)(2,1)} %bitcast.41), dimensions={0,1,3,4} | broadcast | bytes 13762560 | tf_op jit(solution)/shard_map/broadcast_in_dim | solution.py:37
  44.5 255.4 %all_to_all.10 = bf16[2,64,12,3584]{3,0,2,1:T(2,128)(2,1)S(1)} all-to-all(bf16[2,64,12,3584]{3,0,2,1:T(2,128)(2,1)S(1)} %bitcast.40), channel_id=1, replica_groups=mesh['rep'=4,'node'=8,'local'=8] {'node','local'}, dimensions={1} | all-to-all | bytes 22020096 | tf_op jit(solution)/shard_map/all_to_all | solution.py:40
  299.9 68.2 %slice_reduce_fusion = (bf16[64,12,3584]{2,1,0:T(8,128)(2,1)}, bf16[64,12,3584]{2,1,0:T(8,128)(2,1)}) fusion(bf16[2,64,12,3584]{3,0,2,1:T(2,128)(2,1)S(1)} %all_to_all.10), kind=kLoop, calls=%fused_computation.2 | loop fusion | bytes 22020096 | tf_op jit(solution)/shard_map/slice | solution.py:43
  368.1 9.4 %reshape_squeeze.7 = bf16[768,3584]{1,0:T(8,128)(2,1)} reshape(bf16[64,12,3584]{2,1,0:T(8,128)(2,1)} %get-tuple-element.16) | data formatting | bytes 11010048 | tf_op jit(solution)/shard_map/reshape;squeeze | solution.py:43
  377.5 9.5 %reshape_squeeze.6 = bf16[768,3584]{1,0:T(8,128)(2,1)} reshape(bf16[64,12,3584]{2,1,0:T(8,128)(2,1)} %get-tuple-element.17) | data formatting | bytes 11010048 | tf_op jit(solution)/shard_map/reshape;squeeze | solution.py:44
  387.0 4.9 fusion.13
  391.9 1.6 fusion.3
  393.7 1.9 multiply_convert_fusion.3
  395.6 1.6 convolution_convert_fusion.2
  397.2 4.5 convolution_convert_fusion.1
  401.7 4.9 convolution_convert_fusion
  406.6 12.2 %convert_element_type.50 = bf16[64,4,3,3584]{3,2,1,0:T(4,128)(2,1)} reshape(bf16[768,3584]{1,0:T(8,128)(2,1)} %convolution_convert_fusion) | data formatting | bytes 11010048 | tf_op jit(solution)/shard_map/convert_element_type | solution.py:84
  418.8 7.8 %copy.21 = bf16[64,4,3,3584]{3,1,2,0:T(4,128)(2,1)} copy(bf16[64,4,3,3584]{3,2,1,0:T(4,128)(2,1)} %convert_element_type.50) | data formatting | bytes 11010048 | tf_op jit(solution)/shard_map/convert_element_type | solution.py:84
  426.6 5.8 %all-to-all-start.1 = ((bf16[64,4,3,3584]{3,1,2,0:T(4,128)(2,1)}), bf16[64,4,3,3584]{3,1,2,0:T(4,128)(2,1)}, u32[]{:S(2)}, u32[]{:S(2)}) async-start(bf16[64,4,3,3584]{3,1,2,0:T(4,128)(2,1)} %copy.21), calls=%async_computation.1 | async-start | bytes 11010048 | tf_op jit(solution)/shard_map/all_to_all | solution.py:83
  432.5 4.8 pad_maximum_fusion
  437.3 8.1 %copy.27 = bf16[3584,768]{1,0:T(8,128)(2,1)} copy(bf16[3584,768]{0,1:T(8,128)(2,1)} %pad_maximum_fusion) | data formatting | bytes 11010048
  445.5 109.0 %all-to-all-done.1 = bf16[64,4,3,3584]{3,1,2,0:T(4,128)(2,1)} async-done(((bf16[64,4,3,3584]{3,1,2,0:T(4,128)(2,1)}), bf16[64,4,3,3584]{3,1,2,0:T(4,128)(2,1)}, u32[]{:S(2)}, u32[]{:S(2)}) %all-to-all-start.1) | async-done | bytes 5505056 | tf_op jit(solution)/shard_map/all_to_all | solution.py:83
  554.4 5.9 %bitcast_reduce_fusion = bf16[16,4,3,3584]{3,1,2,0:T(4,128)(2,1)S(1)} fusion(bf16[64,4,3,3584]{3,1,2,0:T(4,128)(2,1)} %all-to-all-done.1), kind=kLoop, calls=%fused_computation.7 | loop fusion | flops 2064384 | bytes 6881280
  560.6 0.8 copy.23
  561.7 2.0 gather_fusion
  563.8 2.2 fusion.16
  565.9 1.3 copy.31
  567.2 1.0 copy.24
  568.4 1.0 copy.25
  569.4 1.0 copy.33
  (24 shorter events, 2.0 us)
Async XLA Ops:
  7.2 384.7 %copy-start = (bf16[1,256,3584]{2,1,0:T(8,128)(2,1)S(1)}, bf16[1,256,3584]{2,1,0:T(8,128)(2,1)}, u32[]{:S(2)}) copy-start(bf16[1,256,3584]{2,1,0:T(8,128)(2,1)} %param.13) | copy-start | bytes 5505028
  377.5 16.0 %slice-start = ((s8[5505024]{0:T(1024)(128)(4,1)}), s8[1310720]{0:T(1024)(128)(4,1)S(1)}, s32[]{:S(2)}) async-start(s8[5505024]{0:T(1024)(128)(4,1)} %bitcast.42), calls=%async_computation.4 | async-start | bytes 2621440
  387.0 4.9 copy-start.2
  387.0 6.6 %slice-start.1 = ((s8[5505024]{0:T(1024)(128)(4,1)}), s8[4194304]{0:T(1024)(128)(4,1)S(1)}, s32[]{:S(2)}) async-start(s8[5505024]{0:T(1024)(128)(4,1)} %bitcast.42), calls=%async_computation.5 | async-start | bytes 8388608
  391.9 1.8 copy-start.4
  397.2 4.5 copy-start.3
  426.6 127.9 %all-to-all-start.1 = ((bf16[64,4,3,3584]{3,1,2,0:T(4,128)(2,1)}), bf16[64,4,3,3584]{3,1,2,0:T(4,128)(2,1)}, u32[]{:S(2)}, u32[]{:S(2)}) async-start(bf16[64,4,3,3584]{3,1,2,0:T(4,128)(2,1)} %copy.21), calls=%async_computation.1 | async-start | bytes 11010048 | tf_op jit(solution)/shard_map/all_to_all | solution.py:83
  432.4 131.3 %reduce-scatter.4.cloned.1.call-start = ((), (), s32[]{:S(2)}) async-start(), calls=%async_computation.3 | async-start | bytes 6881280
  561.7 8.7 %copy-start.1 = (bf16[1,256,3584]{2,1,0:T(8,128)(2,1)S(1)}, bf16[1,256,3584]{2,1,0:T(8,128)(2,1)}, u32[]{:S(2)}) copy-start(bf16[1,256,3584]{2,1,0:T(8,128)(2,1)} %param.13) | copy-start | bytes 5505028
Sparse Core Ops, SparseCore 0:
  445.6 60.9 reduce-scatter.3
where the time goes:
time: 580 us; the launch traced here: 577 us
  blocking collectives  255 us (44%)
  local copies, waits for them, and re-layouts  157 us (27%)
  waiting for transfers between devices  109 us (19%)
  matrix products  19.4 us (3%)
  other arithmetic  16 us (3%)
  between operations  14.2 us (2%)
  starting transfers between devices  5.88 us (1%)
    all_to_all x1, blocking collectives, on_device(): lax.all_to_all(copies, ('node', 'local'), split_axis=1, concat_axis=1, ti...  255 us
    all_to_all x1, waiting for transfers between devices, on_device(): lax.all_to_all(shares.astype(jnp.bfloat16), ('node', 'local'), split_axis...  109 us
    slice x1, local copies, waits for them, and re-layouts, on_device(): inputs = arrived[0].reshape(cap_rows, model_width)  68.2 us
    convert_element_type x2, local copies, waits for them, and re-layouts, on_device(): shares.astype(jnp.bfloat16)  20 us
    scatter x1, local copies, waits for them, and re-layouts, on_device(): outgoing = jnp.zeros((2, experts * slots, model_width), jnp.bfloat16).at[...  17.5 us
    unnamed x21, local copies, waits for them, and re-layouts  13.1 us
  transfers between devices with their start and end apart: 2, of which 1 were waited for; matrix products, arithmetic and copies ran while one was open for 4% of the time, Pallas kernels for 0%

commit v1 on v0

v1 whole, which is shorter than its diff:
```python
import jax
import jax.numpy as jnp
from jax import lax
from jax.experimental import pallas as pl
from jax.experimental.pallas import tpu as pltpu
from jax.sharding import PartitionSpec as P

MESH = pl.DeviceIdType.MESH
BF = jnp.bfloat16
F32 = jnp.float32

D = 3584
HALF = D // 2
QUART = D // 4
F = 256
T = 128
NZ = 8
SLOT = 24
UNIT = 2 * SLOT
NT_ROWS = (((1,), (1,)), ((), ()))


def offset_of(k):
    return ((k + 1) // 2) * (1 - 2 * ((k + 1) % 2))


def kernel(
    tok_hbm, grad_hbm, gate_ref, route_ref, wg_hbm, wu_hbm, wd_hbm,
    gt_ref, gw_ref,
    stage, meta, out, x, wg, wu, wd, gp, at, part, rda, rdb, ry, ret, w, ar, br, fin_send, fin_recv, place,
    loc, ex_s, ex_r, z_s, z_r, y_s, y_r, d1_s, d1_r, d2_s, d2_r,
    ra_s, ra_r, rb_s, rb_r, ryy_s, ryy_r, h_s, h_r, rs_s, rs_r, f_s, f_r,
):
    r = lax.axis_index("rep")
    z = lax.axis_index("node")
    l = lax.axis_index("local")
    y = l // 2
    c = l % 2
    pair = y // 2
    core_peer = (r, z, y * 2 + 1 - c)
    y_peer = (r, z, (y + 1 - 2 * (y % 2)) * 2 + c)
    x_next = ((r + 1) % 4, z, l)
    x_prev = ((r + 3) % 4, z, l)
    same = 1 - (pair + c) % 2
    far = 3 - y
    dest_l = same * (y * 2 + 1 - c) + (1 - same) * (far * 2 + c)
    src_l = (1 - same) * (y * 2 + pair) + same * (far * 2 + pair)

    def dest(k):
        return (r, (z + offset_of(k) + NZ) % NZ, dest_l)

    def source(k):
        return (r, (z - offset_of(k) + NZ) % NZ, src_l)

    def rcopy(src, dst, s, q, dev):
        return pltpu.make_async_remote_copy(
            src_ref=src, dst_ref=dst, send_sem=s, recv_sem=q, device_id=dev, device_id_type=MESH
        )

    mine = pl.ds(pl.multiple_of(c * T, T), T)
    mine_g = pl.ds(pl.multiple_of(2 * T + c * T, T), T)
    local = [
        pltpu.make_async_copy(tok_hbm, stage.at[mine], loc.at[0]),
        pltpu.make_async_copy(grad_hbm, stage.at[mine_g], loc.at[1]),
        pltpu.make_async_copy(wg_hbm, wg, loc.at[2]),
        pltpu.make_async_copy(wu_hbm, wu, loc.at[3]),
        pltpu.make_async_copy(wd_hbm, wd, loc.at[4]),
    ]
    for copy in local:
        copy.start()
    row8 = lax.broadcasted_iota(jnp.int32, (8, T), 0)
    meta[c] = jnp.where(row8 == 0, route_ref[...].astype(F32), gate_ref[...])

    barrier = pltpu.get_barrier_semaphore()
    for dev in (core_peer, y_peer, x_next, x_prev):
        pl.semaphore_signal(barrier, inc=1, device_id=dev, device_id_type=MESH)

    def greet(k, carry):
        pl.semaphore_signal(barrier, inc=1, device_id=dest(k), device_id_type=MESH)
        pl.semaphore_signal(barrier, inc=1, device_id=source(k), device_id_type=MESH)
        return carry

    lax.fori_loop(0, NZ, greet, 0)
    pl.semaphore_wait(barrier, 4 + 2 * NZ)

    exchange = [
        rcopy(meta.at[c], meta.at[c], ex_s.at[0], ex_r.at[0], core_peer),
        rcopy(tok_hbm, stage.at[mine], ex_s.at[1], ex_r.at[1], core_peer),
        rcopy(grad_hbm, stage.at[mine_g], ex_s.at[2], ex_r.at[2], core_peer),
    ]
    for copy in exchange:
        copy.start()
    exchange[0].wait_recv()
    route = jnp.concatenate([meta[0, 0:1, :], meta[1, 0:1, :]], axis=1)
    gate = jnp.concatenate([meta[0, 1:2, :], meta[1, 1:2, :]], axis=1)
    expert = lax.broadcasted_iota(jnp.int32, (16, 2 * T), 0)
    wanted = jnp.where(expert < NZ, 2 * expert + c, -1).astype(F32)
    match = jnp.where(route == wanted, 1.0, 0.0)
    earlier = lax.broadcasted_iota(jnp.int32, (2 * T, 2 * T), 0) < lax.broadcasted_iota(
        jnp.int32, (2 * T, 2 * T), 1
    )
    before = jnp.dot(
        match.astype(BF), jnp.where(earlier, 1.0, 0.0).astype(BF), preferred_element_type=F32
    )
    position = jnp.sum(before * match, axis=0, keepdims=True)
    number = jnp.sum(expert.astype(F32) * match, axis=0, keepdims=True)
    known = jnp.sum(match, axis=0, keepdims=True) > 0.5
    target = jnp.where(known, number * SLOT + position, -1.0)
    place[...] = jnp.broadcast_to(jnp.where(known, number * UNIT + position, -1000.0), (8, 2 * T))
    slots = lax.broadcasted_iota(jnp.int32, (NZ * SLOT, 2 * T), 0).astype(F32)
    chosen = slots == target
    slot_gate = jnp.sum(jnp.where(chosen, gate, 0.0), axis=1, keepdims=True)
    pick = jnp.where(chosen, 1.0, 0.0).astype(BF)
    local[0].wait()
    local[1].wait()
    exchange[1].wait_recv()
    exchange[2].wait_recv()

    def pack(i, carry):
        cols = pl.ds(pl.multiple_of(i * 512, 512), 512)
        rows = jnp.dot(pick, stage[0 : 2 * T, cols], preferred_element_type=F32)
        ups = jnp.dot(pick, stage[2 * T : 4 * T, cols], preferred_element_type=F32) * slot_gate
        both = jnp.concatenate(
            [rows.reshape(NZ, SLOT, 512), ups.reshape(NZ, SLOT, 512)], axis=1
        )
        out[:, :, cols] = both.astype(BF)
        return carry

    lax.fori_loop(0, D // 512, pack, 0)

    def send_unit(k):
        return rcopy(
            out.at[(z + offset_of(k) + NZ) % NZ], x.at[k, 0], z_s.at[k], z_r.at[k], dest(k)
        )

    def fwd_y(k):
        return rcopy(x.at[k, 0], x.at[k, 2], y_s.at[k], y_r.at[k], y_peer)

    def fwd_d1(k):
        return rcopy(x.at[k, 0], x.at[k, 1], d1_s.at[k], d1_r.at[k], core_peer)

    def fwd_d2(k):
        return rcopy(x.at[k, 2], x.at[k, 3], d2_s.at[k], d2_r.at[k], core_peer)

    def send_one(k, carry):
        send_unit(k).start()
        return carry

    lax.fori_loop(0, NZ, send_one, 0)
    for copy in local[2:]:
        copy.wait()

    def forward_group(g):
        units = x.at[pl.ds(2 * g, 2)]
        rows = units[...].reshape(8 * UNIT, D)
        pre_g = jnp.dot(rows, wg[...], preferred_element_type=F32)
        pre_u = jnp.dot(rows, wu[...], preferred_element_type=F32)
        gh = lax.dot_general(rows, wd[...], NT_ROWS, preferred_element_type=F32)
        a = pre_g.reshape(8, UNIT, F)[:, :SLOT]
        u = pre_u.reshape(8, UNIT, F)[:, :SLOT]
        h = gh.reshape(8, UNIT, F)[:, SLOT:]
        sigma = 1.0 / (1.0 + jnp.exp(-a))
        swish = a * sigma
        hidden = swish * u
        d_gate = h * u * sigma * (1.0 + a * (1.0 - sigma))
        d_up = h * swish
        gp[pl.ds(pl.multiple_of(g * 192, 64), 192), 0:F] = d_gate.reshape(192, F).astype(BF)
        gp[pl.ds(pl.multiple_of(g * 192, 64), 192), F : 2 * F] = d_up.reshape(192, F).astype(BF)
        zero = jnp.zeros_like(a)
        cols = pl.ds(pl.multiple_of(g * 384, 128), 384)

        def put(first, rest, top):
            both = jnp.concatenate([first, rest], axis=1).reshape(8 * UNIT, F)
            at[top : top + F, cols] = both.T.astype(BF)

        put(d_gate, zero, 0)
        put(d_up, zero, F)
        put(zero, hidden, 2 * F)

    def send_ra(k):
        return rcopy(part.at[k, 1], rda.at[k], ra_s.at[k], ra_r.at[k], core_peer)

    def send_rb(k):
        return rcopy(part.at[k, 3], rdb.at[k], rb_s.at[k], rb_r.at[k], core_peer)

    def route_group(g):
        rows = pl.ds(pl.multiple_of(g * 192, 64), 192)
        left = gp[rows, 0:F]
        right = gp[rows, F : 2 * F]

        def columns(i, carry):
            done = []
            for half in range(2):
                cols = pl.ds(pl.multiple_of(half * HALF + i * 256, 256), 256)
                one = lax.dot_general(left, wg[cols, :], NT_ROWS, preferred_element_type=F32)
                one += lax.dot_general(right, wu[cols, :], NT_ROWS, preferred_element_type=F32)
                done.append(one.reshape(2, 4, SLOT, 256))
            part[pl.ds(2 * g, 2), :, :, pl.ds(pl.multiple_of(i * 256, 256), 256)] = (
                jnp.concatenate(done, axis=2).astype(BF)
            )
            return carry

        lax.fori_loop(0, HALF // 256, columns, 0)
        for kk in range(2):
            send_ra(2 * g + kk).start()
            send_rb(2 * g + kk).start()

    def turn(i, carry):
        @pl.when(i < 4)
        def _():
            for kk in range(2):
                k = 2 * i + kk
                send_unit(k).wait_recv()
                fwd_y(k).start()
                fwd_d1(k).start()

        @pl.when(i > 0)
        def _():
            for kk in range(2):
                k = 2 * i - 2 + kk
                fwd_y(k).wait_recv()
                fwd_d2(k).start()
            for kk in range(2):
                k = 2 * i - 2 + kk
                fwd_d1(k).wait_recv()
                fwd_d2(k).wait_recv()
            forward_group(i - 1)

        @pl.when((i > 0) & (i < 4))
        def _():
            route_group(i - 1)

        return carry

    lax.fori_loop(0, 5, turn, 0)

    def weight_chunk(q):
        cols = pl.ds(pl.multiple_of(q * QUART, 128), QUART)
        rows = x[:, :, :, cols].reshape(32 * UNIT, QUART)

        def block(m, carry):
            these = pl.ds(pl.multiple_of(m * 256, 256), 256)
            w[q, these, :] = jnp.dot(at[these, :], rows, preferred_element_type=F32).astype(BF)
            return carry

        lax.fori_loop(0, 3, block, 0)

    opposite, nxt, prv = (r + 2) % 4, (r + 1) % 4, (r + 3) % 4
    low, high = pl.ds(0, 384), pl.ds(384, 384)
    reduce = [
        rcopy(w.at[opposite, low], ar.at[0], rs_s.at[0], rs_r.at[0], x_next),
        rcopy(w.at[opposite, high], ar.at[1], rs_s.at[1], rs_r.at[1], x_prev),
        rcopy(w.at[nxt, high], br.at[0, high], rs_s.at[2], rs_r.at[2], x_next),
        rcopy(w.at[prv, low], br.at[1, low], rs_s.at[3], rs_r.at[3], x_prev),
        rcopy(w.at[nxt, low], br.at[0, low], rs_s.at[4], rs_r.at[4], x_next),
        rcopy(w.at[prv, high], br.at[1, high], rs_s.at[5], rs_r.at[5], x_prev),
    ]

    def step(j, carry):
        weight_chunk((r + 2 + j + (j // 2)) % 4)

        @pl.when(j == 0)
        def _():
            reduce[0].start()
            reduce[1].start()

        @pl.when(j == 1)
        def _():
            reduce[3].start()

        @pl.when(j == 2)
        def _():
            reduce[2].start()

        @pl.when(j == 2)
        def _():
            route_group(3)

        return carry

    lax.fori_loop(0, 3, step, 0)

    def across(k, carry):
        send_rb(k).wait_recv()
        part[k, 2] = (part[k, 2].astype(F32) + rdb[k].astype(F32)).astype(BF)
        rcopy(part.at[k, 2], ry.at[k], ryy_s.at[k], ryy_r.at[k], y_peer).start()
        return carry

    lax.fori_loop(0, NZ, across, 0)

    weight_chunk(r)

    reduce[0].wait_recv()
    w[nxt, 0:384, :] = (w[nxt, 0:384, :].astype(F32) + ar[0].astype(F32)).astype(BF)
    reduce[4].start()
    reduce[1].wait_recv()
    w[prv, 384:768, :] = (w[prv, 384:768, :].astype(F32) + ar[1].astype(F32)).astype(BF)
    reduce[5].start()

    def send_home(k):
        return rcopy(part.at[k, 0], ret.at[z], h_s.at[k], h_r.at[z], source(k))

    def home(k, carry):
        send_ra(k).wait_recv()
        rcopy(part.at[k, 2], ry.at[k], ryy_s.at[k], ryy_r.at[k], y_peer).wait_recv()
        part[k, 0] = (
            part[k, 0].astype(F32) + rda[k].astype(F32) + ry[k].astype(F32)
        ).astype(BF)
        send_home(k).start()
        return carry

    lax.fori_loop(0, NZ, home, 0)

    def arrived(j, carry):
        rcopy(part.at[j, 0], ret.at[j], h_s.at[j], h_r.at[j], source(0)).wait_recv()
        return carry

    lax.fori_loop(0, NZ, arrived, 0)

    unit_rows = lax.broadcasted_iota(jnp.int32, (NZ * UNIT, 2 * T), 0).astype(F32)

    def last(i, carry):
        cols = pl.ds(pl.multiple_of(i * 256, 256), 256)
        rows = ret[:, :, cols].reshape(NZ * UNIT, 256)
        for half in range(2):
            pick_t = jnp.where(unit_rows == place[0:1, :] + half * SLOT, 1.0, 0.0).astype(BF)
            got = lax.dot_general(
                pick_t, rows, (((0,), (0,)), ((), ())), preferred_element_type=F32
            )
            both = got.reshape(2, T, 256).astype(BF)
            outc = pl.ds(pl.multiple_of(half * HALF + i * 256, 256), 256)
            fin_send[:, :, outc] = both
        return carry

    lax.fori_loop(0, HALF // 256, last, 0)
    final = rcopy(fin_send.at[1 - c], fin_recv, f_s, f_r, core_peer)
    final.start()
    final.wait_recv()
    gt_ref[...] = (fin_send[c].astype(F32) + fin_recv[...].astype(F32)).astype(BF)

    for j in (2, 3, 4, 5):
        reduce[j].wait_recv()
    gw_ref[...] = (
        w[r].astype(F32) + br[0].astype(F32) + br[1].astype(F32)
    ).astype(BF)

    for copy in exchange + reduce + [final]:
        copy.wait_send()

    def drain(k, carry):
        send_unit(k).wait_send()
        fwd_y(k).wait_send()
        fwd_d1(k).wait_send()
        fwd_d2(k).wait_send()
        send_ra(k).wait_send()
        send_rb(k).wait_send()
        rcopy(part.at[k, 2], ry.at[k], ryy_s.at[k], ryy_r.at[k], y_peer).wait_send()
        send_home(k).wait_send()
        return carry

    lax.fori_loop(0, NZ, drain, 0)


def on_device(tokens, grad_out, gates, routes, w_gate, w_up, w_down):
    dma = pltpu.SemaphoreType.DMA
    vmem = pl.BlockSpec(memory_space=pltpu.VMEM)
    anyspace = pl.BlockSpec(memory_space=pl.ANY)
    flops = 2 * 1536 * D * F * 7
    grad_tokens, grads = pl.pallas_call(
        kernel,
        out_shape=(
            jax.ShapeDtypeStruct((T, D), BF),
            jax.ShapeDtypeStruct((3 * F, QUART), BF),
        ),
        in_specs=[anyspace, anyspace, vmem, vmem, anyspace, anyspace, anyspace],
        out_specs=(vmem, vmem),
        scratch_shapes=[
            pltpu.VMEM((4 * T, D), BF),
            pltpu.VMEM((2, 8, T), F32),
            pltpu.VMEM((NZ, UNIT, D), BF),
            pltpu.VMEM((NZ, 4, UNIT, D), BF),
            pltpu.VMEM((D, F), BF),
            pltpu.VMEM((D, F), BF),
            pltpu.VMEM((F, D), BF),
            pltpu.VMEM((768, 2 * F), BF),
            pltpu.VMEM((3 * F, 32 * UNIT), BF),
            pltpu.VMEM((NZ, 4, UNIT, HALF), BF),
            pltpu.VMEM((NZ, UNIT, HALF), BF),
            pltpu.VMEM((NZ, UNIT, HALF), BF),
            pltpu.VMEM((NZ, UNIT, HALF), BF),
            pltpu.VMEM((NZ, UNIT, HALF), BF),
            pltpu.VMEM((4, 3 * F, QUART), BF),
            pltpu.VMEM((2, 384, QUART), BF),
            pltpu.VMEM((2, 3 * F, QUART), BF),
            pltpu.VMEM((2, T, D), BF),
            pltpu.VMEM((T, D), BF),
            pltpu.VMEM((8, 2 * T), F32),
            dma((5,)), dma((3,)), dma((3,)),
            dma((NZ,)), dma((NZ,)), dma((NZ,)), dma((NZ,)),
            dma((NZ,)), dma((NZ,)), dma((NZ,)), dma((NZ,)),
            dma((NZ,)), dma((NZ,)), dma((NZ,)), dma((NZ,)),
            dma((NZ,)), dma((NZ,)), dma((NZ,)), dma((NZ,)),
            dma((6,)), dma((6,)), dma, dma,
        ],
        compiler_params=pltpu.CompilerParams(
            collective_id=0, has_side_effects=True, vmem_limit_bytes=62 * 1024 * 1024
        ),
        cost_estimate=pl.CostEstimate(flops=flops, bytes_accessed=10_000_000, transcendentals=0),
    )(
        tokens, grad_out, gates.reshape(1, T), routes.reshape(1, T),
        w_gate[0], w_up[0], w_down[0],
    )
    return (
        grad_tokens,
        grads[:F].T[None],
        grads[F : 2 * F].T[None],
        grads[2 * F :][None],
    )


def solution(mesh):
    in_specs = (
        P(("rep", "node", "local"), None),
        P(("rep", "node", "local"), None),
        P(("rep", "node", "local"), None),
        P(("rep", "node", "local"), None),
        P(("node", "local"), None, None),
        P(("node", "local"), None, None),
        P(("node", "local"), None, None),
    )
    out_specs = (
        P(("rep", "node", "local"), None),
        P(("node", "local"), "rep", None),
        P(("node", "local"), "rep", None),
        P(("node", "local"), None, "rep"),
    )
    return jax.shard_map(
        on_device, mesh=mesh, in_specs=in_specs, out_specs=out_specs, check_vma=False
    )
```

time: 580 us -> 170 us (0.29)
  the two profiles are of different devices: /device:TPU:1 before, /device:TPU:192 now
where the time goes in v1:
time: 170 us
  Pallas kernels  164 us (96%)
  local copies, waits for them, and re-layouts  5.15 us (3%)
    pallas_call x1, Pallas kernels, on_device(): pl.pallas_call(kernel, out_shape=(jax.ShapeDtypeStruct((T, D), BF), jax.S...  164 us

profile of v1, /device:TPU:192, one launch (start us, length us, event | category | flops | bytes accessed | tf_op | source)
XLA Modules:
  0.0 169.5 jit_solution(15234162508599555120)
XLA Ops:
  0.6 163.7 %shard_map.102 = (bf16[128,3584]{1,0:T(8,128)(2,1)}, bf16[768,896]{1,0:T(8,128)(2,1)}) custom-call(bf16[128,3584]{1,0:T(8,128)(2,1)} %tok_hbm.1, bf16[128,3584]{1,0:T(8,128)(2,1)} %grad_hbm.1, f32[1,128]{1,0:T(1,128)} %bitcast.18, s32[1,128]{1,0:T(1,128)} %bitcast.19, bf16[3584,256]{1,0:T(8,128)(2,1)} %bitcast.15, bf16[3584,256]{1,0:T(8,128)(2,1)} %bitcast.16, ...), custom_call_target="tpu_custom_call" | custom-call | flops 19730006016 | bytes 10000000 | tf_op jit(solution)/shard_map/pallas_call | solution.py:369
  164.4 0.0 copy-start
  164.4 2.3 %slice_bitcast_fusion = (bf16[1,256,896]{2,1,0:T(8,128)(2,1)}, bf16[1,896,256]{1,2,0:T(8,128)(2,1)S(1)}, bf16[1,896,256]{1,2,0:T(8,128)(2,1)S(1)}) fusion(bf16[768,896]{1,0:T(8,128)(2,1)} %get-tuple-element.7), kind=kLoop, calls=%fused_computation | loop fusion | bytes 2752512 | tf_op jit(solution)/shard_map/broadcast_in_dim | solution.py:417
  166.6 1.0 copy.12
  167.6 1.0 copy.11
  168.6 0.0 copy-done
  168.6 0.9 copy.14
Async XLA Ops:
  164.4 4.2 %copy-start = (bf16[128,3584]{1,0:T(8,128)(2,1)S(1)}, bf16[128,3584]{1,0:T(8,128)(2,1)}, u32[]{:S(2)}) copy-start(bf16[128,3584]{1,0:T(8,128)(2,1)} %get-tuple-element.19) | copy-start | bytes 2752516

commit v2 on v1

--- a/solution.py
+++ b/solution.py
@@ -27,9 +27,11 @@
 def kernel(
     tok_hbm, grad_hbm, gate_ref, route_ref, wg_hbm, wu_hbm, wd_hbm,
     gt_ref, gw_ref,
-    stage, meta, out, x, wg, wu, wd, gp, at, part, rda, rdb, ry, ret, w, ar, br, fin_send, fin_recv, place,
+    stage, meta, out, x, wg, wu, wd, at, part, rda, rdb, ry, ret, w, ar, br, fin_send, fin_recv, place,
+    xt, xq, gall, acc,
     loc, ex_s, ex_r, z_s, z_r, y_s, y_r, d1_s, d1_r, d2_s, d2_r,
     ra_s, ra_r, rb_s, rb_r, ryy_s, ryy_r, h_s, h_r, rs_s, rs_r, f_s, f_r,
+    xs_s, xs_r, xc_s, xc_r, gs_s, gs_r,
 ):
     r = lax.axis_index("rep")
     z = lax.axis_index("node")
@@ -41,6 +43,7 @@
     y_peer = (r, z, (y + 1 - 2 * (y % 2)) * 2 + c)
     x_next = ((r + 1) % 4, z, l)
     x_prev = ((r + 3) % 4, z, l)
+    x_far = ((r + 2) % 4, z, l)
     same = 1 - (pair + c) % 2
     far = 3 - y
     dest_l = same * (y * 2 + 1 - c) + (1 - same) * (far * 2 + c)
@@ -72,7 +75,7 @@
     meta[c] = jnp.where(row8 == 0, route_ref[...].astype(F32), gate_ref[...])
 
     barrier = pltpu.get_barrier_semaphore()
-    for dev in (core_peer, y_peer, x_next, x_prev):
+    for dev in (core_peer, y_peer, x_next, x_prev, x_far):
         pl.semaphore_signal(barrier, inc=1, device_id=dev, device_id_type=MESH)
 
     def greet(k, carry):
@@ -81,7 +84,7 @@
         return carry
 
     lax.fori_loop(0, NZ, greet, 0)
-    pl.semaphore_wait(barrier, 4 + 2 * NZ)
+    pl.semaphore_wait(barrier, 5 + 2 * NZ)
 
     exchange = [
         rcopy(meta.at[c], meta.at[c], ex_s.at[0], ex_r.at[0], core_peer),
@@ -134,13 +137,13 @@
         )
 
     def fwd_y(k):
-        return rcopy(x.at[k, 0], x.at[k, 2], y_s.at[k], y_r.at[k], y_peer)
+        return rcopy(x.at[k, 0], x.at[k, 1], y_s.at[k], y_r.at[k], y_peer)
 
     def fwd_d1(k):
-        return rcopy(x.at[k, 0], x.at[k, 1], d1_s.at[k], d1_r.at[k], core_peer)
+        return rcopy(x.at[k, 0], x.at[k, 2], d1_s.at[k], d1_r.at[k], core_peer)
 
     def fwd_d2(k):
-        return rcopy(x.at[k, 2], x.at[k, 3], d2_s.at[k], d2_r.at[k], core_peer)
+        return rcopy(x.at[k, 1], x.at[k, 3], d2_s.at[k], d2_r.at[k], core_peer)
 
     def send_one(k, carry):
         send_unit(k).start()
@@ -164,29 +167,86 @@
         hidden = swish * u
         d_gate = h * u * sigma * (1.0 + a * (1.0 - sigma))
         d_up = h * swish
-        gp[pl.ds(pl.multiple_of(g * 192, 64), 192), 0:F] = d_gate.reshape(192, F).astype(BF)
-        gp[pl.ds(pl.multiple_of(g * 192, 64), 192), F : 2 * F] = d_up.reshape(192, F).astype(BF)
-        zero = jnp.zeros_like(a)
+        gall[g, 0, :, 0:F] = d_gate.reshape(192, F).astype(BF)
+        gall[g, 0, :, F : 2 * F] = d_up.reshape(192, F).astype(BF)
         cols = pl.ds(pl.multiple_of(g * 384, 128), 384)
-
-        def put(first, rest, top):
-            both = jnp.concatenate([first, rest], axis=1).reshape(8 * UNIT, F)
-            at[top : top + F, cols] = both.T.astype(BF)
-
-        put(d_gate, zero, 0)
-        put(d_up, zero, F)
-        put(zero, hidden, 2 * F)
+        both = jnp.concatenate([jnp.zeros_like(hidden), hidden], axis=1).reshape(8 * UNIT, F)
+        at[:, cols] = both.T.astype(BF)
+
+    def quarter(q):
+        return pl.ds(pl.multiple_of(q * QUART, 128), QUART)
+
+    def xt_send(k, j):
+        return rcopy(
+            xt.at[k, :, quarter((r + j) % 4)], xq.at[k // 2, 4 - j, k % 2, 0],
+            xs_s.at[k, j], xs_r.at[k, 4 - j], ((r + j) % 4, z, l),
+        )
+
+    def xt_got(k, j):
+        return rcopy(
+            xt.at[k, :, quarter(r)], xq.at[k // 2, j, k % 2, 0],
+            xs_s.at[k, j], xs_r.at[k, j], ((r + j) % 4, z, l),
+        )
+
+    def xq_fwd(k, j):
+        src = xt.at[k, :, quarter(r)] if j == 0 else xq.at[k // 2, j, k % 2, 0]
+        return rcopy(src, xq.at[k // 2, j, k % 2, 1], xc_s.at[k, j], xc_r.at[k, j], core_peer)
+
+    def g_send(g, j):
+        return rcopy(
+            gall.at[g, 0], gall.at[g, 4 - j], gs_s.at[g, j], gs_r.at[g, 4 - j], ((r + j) % 4, z, l)
+        )
+
+    def g_got(g, j):
+        return rcopy(gall.at[g, 0], gall.at[g, j], gs_s.at[g, j], gs_r.at[g, j], ((r + j) % 4, z, l))
+
+    def compact(k):
+        def columns(i, carry):
+            cols = pl.ds(pl.multiple_of(i * QUART, 128), QUART)
+            both = x[k, 0:2, :, cols].astype(F32)[:, :SLOT]
+            xt[k, :, cols] = both.reshape(UNIT, QUART).astype(BF)
+            return carry
+
+        lax.fori_loop(0, 4, columns, 0)
+        xq[k // 2, 0, k % 2, 0] = xt[k, :, quarter(r)]
+        for j in (2, 1, 3):
+            xt_send(k, j).start()
+        xq_fwd(k, 0).start()
+
+    def relay_quarters(g):
+        for kk in range(2):
+            for j in (1, 2, 3):
+                xt_got(2 * g + kk, j).wait_recv()
+                xq_fwd(2 * g + kk, j).start()
+
+    def send_grads(g):
+        for j in (2, 1, 3):
+            g_send(g, j).start()
+
+    def accumulate(g, first):
+        for kk in range(2):
+            for j in range(4):
+                xq_fwd(2 * g + kk, j).wait_recv()
+        for j in (1, 2, 3):
+            g_got(g, j).wait_recv()
+        rows = xq[g].reshape(4 * 192, QUART)
+        for m in range(2):
+            left = gall[g, :, :, m * F : (m + 1) * F].reshape(4 * 192, F)
+            term = lax.dot_general(left, rows, (((0,), (0,)), ((), ())), preferred_element_type=F32)
+            if first:
+                acc[m] = term
+            else:
+                acc[m] += term
 
     def send_ra(k):
-        return rcopy(part.at[k, 1], rda.at[k], ra_s.at[k], ra_r.at[k], core_peer)
+        return rcopy(part.at[k, 2], rda.at[k], ra_s.at[k], ra_r.at[k], core_peer)
 
     def send_rb(k):
         return rcopy(part.at[k, 3], rdb.at[k], rb_s.at[k], rb_r.at[k], core_peer)
 
     def route_group(g):
-        rows = pl.ds(pl.multiple_of(g * 192, 64), 192)
-        left = gp[rows, 0:F]
-        right = gp[rows, F : 2 * F]
+        left = gall[g, 0, :, 0:F]
+        right = gall[g, 0, :, F : 2 * F]
 
         def columns(i, carry):
             done = []
@@ -205,48 +265,83 @@
             send_ra(2 * g + kk).start()
             send_rb(2 * g + kk).start()
 
-    def turn(i, carry):
-        @pl.when(i < 4)
+    def y_return(k):
+        return rcopy(part.at[k, 1], ry.at[k], ryy_s.at[k], ryy_r.at[k], y_peer)
+
+    def across(k):
+        send_rb(k).wait_recv()
+        part[k, 1] = (part[k, 1].astype(F32) + rdb[k].astype(F32)).astype(BF)
+        y_return(k).start()
+
+    def send_home(k):
+        return rcopy(part.at[k, 0], ret.at[z], h_s.at[k], h_r.at[z], source(k))
+
+    def home(k):
+        send_ra(k).wait_recv()
+        y_return(k).wait_recv()
+        part[k, 0] = (
+            part[k, 0].astype(F32) + rda[k].astype(F32) + ry[k].astype(F32)
+        ).astype(BF)
+        send_home(k).start()
+
+    def turn(t, carry):
+        @pl.when(t < NZ)
+        def _():
+            send_unit(t).wait_recv()
+            fwd_y(t).start()
+            fwd_d1(t).start()
+
+        @pl.when(t > 0)
+        def _():
+            k = t - 1
+            fwd_y(k).wait_recv()
+            fwd_d2(k).start()
+            compact(k)
+
+        even = t % 2 == 0
+
+        @pl.when(t == NZ)
+        def _():
+            def early(m, carry):
+                across(5 - m)
+                return carry
+
+            lax.fori_loop(0, 6, early, 0)
+
+        @pl.when((t > 0) & even)
         def _():
             for kk in range(2):
-                k = 2 * i + kk
-                send_unit(k).wait_recv()
-                fwd_y(k).start()
-                fwd_d1(k).start()
-
-        @pl.when(i > 0)
-        def _():
-            for kk in range(2):
-                k = 2 * i - 2 + kk
-                fwd_y(k).wait_recv()
-                fwd_d2(k).start()
-            for kk in range(2):
-                k = 2 * i - 2 + kk
-                fwd_d1(k).wait_recv()
-                fwd_d2(k).wait_recv()
-            forward_group(i - 1)
-
-        @pl.when((i > 0) & (i < 4))
-        def _():
-            route_group(i - 1)
-
-        return carry
-
-    lax.fori_loop(0, 5, turn, 0)
+                fwd_d1(t - 2 + kk).wait_recv()
+                fwd_d2(t - 2 + kk).wait_recv()
+            forward_group(t // 2 - 1)
+
+        @pl.when((t > 0) & (t < NZ) & even)
+        def _():
+            send_grads(t // 2 - 1)
+            route_group(t // 2 - 1)
+
+        @pl.when((t > 3) & even)
+        def _():
+            relay_quarters(t // 2 - 2)
+
+        @pl.when(t == 6)
+        def _():
+            accumulate(0, True)
+
+        @pl.when(t == 8)
+        def _():
+            accumulate(1, False)
+
+        return carry
+
+    lax.fori_loop(0, NZ + 1, turn, 0)
 
     def weight_chunk(q):
-        cols = pl.ds(pl.multiple_of(q * QUART, 128), QUART)
-        rows = x[:, :, :, cols].reshape(32 * UNIT, QUART)
-
-        def block(m, carry):
-            these = pl.ds(pl.multiple_of(m * 256, 256), 256)
-            w[q, these, :] = jnp.dot(at[these, :], rows, preferred_element_type=F32).astype(BF)
-            return carry
-
-        lax.fori_loop(0, 3, block, 0)
+        rows = x[:, :, :, quarter(q)].reshape(32 * UNIT, QUART)
+        w[q] = jnp.dot(at[...], rows, preferred_element_type=F32).astype(BF)
 
     opposite, nxt, prv = (r + 2) % 4, (r + 1) % 4, (r + 3) % 4
-    low, high = pl.ds(0, 384), pl.ds(384, 384)
+    low, high = pl.ds(0, 128), pl.ds(128, 128)
     reduce = [
         rcopy(w.at[opposite, low], ar.at[0], rs_s.at[0], rs_r.at[0], x_next),
         rcopy(w.at[opposite, high], ar.at[1], rs_s.at[1], rs_r.at[1], x_prev),
@@ -263,6 +358,7 @@
         def _():
             reduce[0].start()
             reduce[1].start()
+            send_grads(3)
 
         @pl.when(j == 1)
         def _():
@@ -272,44 +368,40 @@
         def _():
             reduce[2].start()
 
-        @pl.when(j == 2)
-        def _():
-            route_group(3)
-
         return carry
 
     lax.fori_loop(0, 3, step, 0)
-
-    def across(k, carry):
-        send_rb(k).wait_recv()
-        part[k, 2] = (part[k, 2].astype(F32) + rdb[k].astype(F32)).astype(BF)
-        rcopy(part.at[k, 2], ry.at[k], ryy_s.at[k], ryy_r.at[k], y_peer).start()
-        return carry
-
-    lax.fori_loop(0, NZ, across, 0)
-
+    route_group(3)
+
+    def late(m, carry):
+        across(6 + m)
+        return carry
+
+    lax.fori_loop(0, 2, late, 0)
+
+    def first_home(m, carry):
+        home(5 - m)
+        return carry
+
+    lax.fori_loop(0, 3, first_home, 0)
     weight_chunk(r)
+    relay_quarters(3)
+    accumulate(2, False)
 
     reduce[0].wait_recv()
-    w[nxt, 0:384, :] = (w[nxt, 0:384, :].astype(F32) + ar[0].astype(F32)).astype(BF)
+    w[nxt, 0:128, :] = (w[nxt, 0:128, :].astype(F32) + ar[0].astype(F32)).astype(BF)
     reduce[4].start()
     reduce[1].wait_recv()
-    w[prv, 384:768, :] = (w[prv, 384:768, :].astype(F32) + ar[1].astype(F32)).astype(BF)
+    w[prv, 128:256, :] = (w[prv, 128:256, :].astype(F32) + ar[1].astype(F32)).astype(BF)
     reduce[5].start()
 
-    def send_home(k):
-        return rcopy(part.at[k, 0], ret.at[z], h_s.at[k], h_r.at[z], source(k))
-
-    def home(k, carry):
-        send_ra(k).wait_recv()
-        rcopy(part.at[k, 2], ry.at[k], ryy_s.at[k], ryy_r.at[k], y_peer).wait_recv()
-        part[k, 0] = (
-            part[k, 0].astype(F32) + rda[k].astype(F32) + ry[k].astype(F32)
-        ).astype(BF)
-        send_home(k).start()
-        return carry
-
-    lax.fori_loop(0, NZ, home, 0)
+    def second_home(m, carry):
+        home((m < 3) * (2 - m) + (m >= 3) * (m + 3))
+        return carry
+
+    lax.fori_loop(0, 5, second_home, 0)
+    accumulate(3, False)
+    gw_ref[0 : 2 * F, :] = acc[...].reshape(2 * F, QUART).astype(BF)
 
     def arrived(j, carry):
         rcopy(part.at[j, 0], ret.at[j], h_s.at[j], h_r.at[j], source(0)).wait_recv()
@@ -340,7 +432,7 @@
 
     for j in (2, 3, 4, 5):
         reduce[j].wait_recv()
-    gw_ref[...] = (
+    gw_ref[2 * F :, :] = (
         w[r].astype(F32) + br[0].astype(F32) + br[1].astype(F32)
     ).astype(BF)
 
@@ -354,11 +446,18 @@
         fwd_d2(k).wait_send()
         send_ra(k).wait_send()
         send_rb(k).wait_send()
-        rcopy(part.at[k, 2], ry.at[k], ryy_s.at[k], ryy_r.at[k], y_peer).wait_send()
+        y_return(k).wait_send()
         send_home(k).wait_send()
+        for j in range(4):
+            xq_fwd(k, j).wait_send()
+        for j in (1, 2, 3):
+            xt_send(k, j).wait_send()
         return carry
 
     lax.fori_loop(0, NZ, drain, 0)
+    for g in range(4):
+        for j in (1, 2, 3):
+            g_send(g, j).wait_send()
 
 
 def on_device(tokens, grad_out, gates, routes, w_gate, w_up, w_down):
@@ -382,25 +481,29 @@
             pltpu.VMEM((D, F), BF),
             pltpu.VMEM((D, F), BF),
             pltpu.VMEM((F, D), BF),
-            pltpu.VMEM((768, 2 * F), BF),
-            pltpu.VMEM((3 * F, 32 * UNIT), BF),
+            pltpu.VMEM((F, 32 * UNIT), BF),
             pltpu.VMEM((NZ, 4, UNIT, HALF), BF),
             pltpu.VMEM((NZ, UNIT, HALF), BF),
             pltpu.VMEM((NZ, UNIT, HALF), BF),
             pltpu.VMEM((NZ, UNIT, HALF), BF),
             pltpu.VMEM((NZ, UNIT, HALF), BF),
-            pltpu.VMEM((4, 3 * F, QUART), BF),
-            pltpu.VMEM((2, 384, QUART), BF),
-            pltpu.VMEM((2, 3 * F, QUART), BF),
+            pltpu.VMEM((4, F, QUART), BF),
+            pltpu.VMEM((2, 128, QUART), BF),
+            pltpu.VMEM((2, F, QUART), BF),
             pltpu.VMEM((2, T, D), BF),
             pltpu.VMEM((T, D), BF),
             pltpu.VMEM((8, 2 * T), F32),
+            pltpu.VMEM((NZ, UNIT, D), BF),
+            pltpu.VMEM((4, 4, 2, 2, UNIT, QUART), BF),
+            pltpu.VMEM((4, 4, 192, 2 * F), BF),
+            pltpu.VMEM((2, F, QUART), F32),
             dma((5,)), dma((3,)), dma((3,)),
             dma((NZ,)), dma((NZ,)), dma((NZ,)), dma((NZ,)),
             dma((NZ,)), dma((NZ,)), dma((NZ,)), dma((NZ,)),
             dma((NZ,)), dma((NZ,)), dma((NZ,)), dma((NZ,)),
             dma((NZ,)), dma((NZ,)), dma((NZ,)), dma((NZ,)),
             dma((6,)), dma((6,)), dma, dma,
+            dma((NZ, 4)), dma((NZ, 4)), dma((NZ, 4)), dma((NZ, 4)), dma((4, 4)), dma((4, 4)),
         ],
         compiler_params=pltpu.CompilerParams(
             collective_id=0, has_side_effects=True, vmem_limit_bytes=62 * 1024 * 1024

time: 170 us -> 157 us (0.924)
  the two profiles are of different devices: /device:TPU:192 before, /device:TPU:1 now
where the time goes in v2:
time: 157 us
  Pallas kernels  151 us (96%)
  local copies, waits for them, and re-layouts  5.15 us (3%)
    pallas_call x1, Pallas kernels, on_device(): pl.pallas_call(kernel, out_shape=(jax.ShapeDtypeStruct((T, D), BF), jax.S...  151 us

profile of v2, /device:TPU:1, one launch (start us, length us, event | category | flops | bytes accessed | tf_op | source)
XLA Modules:
  0.0 157.2 jit_solution(13438452587084735736)
XLA Ops:
  0.6 151.4 %shard_map.102 = (bf16[128,3584]{1,0:T(8,128)(2,1)}, bf16[768,896]{1,0:T(8,128)(2,1)}) custom-call(bf16[128,3584]{1,0:T(8,128)(2,1)} %tok_hbm.1, bf16[128,3584]{1,0:T(8,128)(2,1)} %grad_hbm.1, f32[1,128]{1,0:T(1,128)} %bitcast.18, s32[1,128]{1,0:T(1,128)} %bitcast.19, bf16[3584,256]{1,0:T(8,128)(2,1)} %bitcast.15, bf16[3584,256]{1,0:T(8,128)(2,1)} %bitcast.16, ...), custom_call_target="tpu_custom_call" | custom-call | flops 19730006016 | bytes 10000000 | tf_op jit(solution)/shard_map/pallas_call | solution.py:468
  152.0 0.0 copy-start
  152.0 2.3 %slice_bitcast_fusion = (bf16[1,256,896]{2,1,0:T(8,128)(2,1)}, bf16[1,896,256]{1,2,0:T(8,128)(2,1)S(1)}, bf16[1,896,256]{1,2,0:T(8,128)(2,1)S(1)}) fusion(bf16[768,896]{1,0:T(8,128)(2,1)} %get-tuple-element.7), kind=kLoop, calls=%fused_computation | loop fusion | bytes 2752512 | tf_op jit(solution)/shard_map/broadcast_in_dim | solution.py:520
  154.3 1.0 copy.12
  155.3 1.0 copy.11
  156.3 0.0 copy-done
  156.3 0.9 copy.14
Async XLA Ops:
  152.0 4.2 %copy-start = (bf16[128,3584]{1,0:T(8,128)(2,1)S(1)}, bf16[128,3584]{1,0:T(8,128)(2,1)}, u32[]{:S(2)}) copy-start(bf16[128,3584]{1,0:T(8,128)(2,1)} %get-tuple-element.19) | copy-start | bytes 2752516

commit v3 on v2

--- a/solution.py
+++ b/solution.py
@@ -26,9 +26,9 @@
 
 def kernel(
     tok_hbm, grad_hbm, gate_ref, route_ref, wg_hbm, wu_hbm, wd_hbm,
-    gt_ref, gw_ref,
+    gt_ref, gg_ref, gu_ref, gd_ref,
     stage, meta, out, x, wg, wu, wd, at, part, rda, rdb, ry, ret, w, ar, br, fin_send, fin_recv, place,
-    xt, xq, gall, acc,
+    xt, xq, gall, acc, hz,
     loc, ex_s, ex_r, z_s, z_r, y_s, y_r, d1_s, d1_r, d2_s, d2_r,
     ra_s, ra_r, rb_s, rb_r, ryy_s, ryy_r, h_s, h_r, rs_s, rs_r, f_s, f_r,
     xs_s, xs_r, xc_s, xc_r, gs_s, gs_r,
@@ -109,7 +109,6 @@
     number = jnp.sum(expert.astype(F32) * match, axis=0, keepdims=True)
     known = jnp.sum(match, axis=0, keepdims=True) > 0.5
     target = jnp.where(known, number * SLOT + position, -1.0)
-    place[...] = jnp.broadcast_to(jnp.where(known, number * UNIT + position, -1000.0), (8, 2 * T))
     slots = lax.broadcasted_iota(jnp.int32, (NZ * SLOT, 2 * T), 0).astype(F32)
     chosen = slots == target
     slot_gate = jnp.sum(jnp.where(chosen, gate, 0.0), axis=1, keepdims=True)
@@ -131,13 +130,20 @@
 
     lax.fori_loop(0, D // 512, pack, 0)
 
-    def send_unit(k):
-        return rcopy(
-            out.at[(z + offset_of(k) + NZ) % NZ], x.at[k, 0], z_s.at[k], z_r.at[k], dest(k)
-        )
-
-    def fwd_y(k):
-        return rcopy(x.at[k, 0], x.at[k, 1], y_s.at[k], y_r.at[k], y_peer)
+    def half_cols(h):
+        return pl.ds(pl.multiple_of(h * HALF, 128), HALF)
+
+    def send_unit(k, h):
+        return rcopy(
+            out.at[(z + offset_of(k) + NZ) % NZ, :, half_cols(h)], x.at[k, 0, :, half_cols(h)],
+            z_s.at[k, h], z_r.at[k, h], dest(k),
+        )
+
+    def fwd_y(k, h):
+        return rcopy(
+            x.at[k, 0, :, half_cols(h)], x.at[k, 1, :, half_cols(h)],
+            y_s.at[k, h], y_r.at[k, h], y_peer,
+        )
 
     def fwd_d1(k):
         return rcopy(x.at[k, 0], x.at[k, 2], d1_s.at[k], d1_r.at[k], core_peer)
@@ -146,32 +152,35 @@
         return rcopy(x.at[k, 1], x.at[k, 3], d2_s.at[k], d2_r.at[k], core_peer)
 
     def send_one(k, carry):
-        send_unit(k).start()
+        send_unit(k, 0).start()
+        send_unit(k, 1).start()
         return carry
 
     lax.fori_loop(0, NZ, send_one, 0)
     for copy in local[2:]:
         copy.wait()
-
-    def forward_group(g):
-        units = x.at[pl.ds(2 * g, 2)]
-        rows = units[...].reshape(8 * UNIT, D)
+    back = jnp.where(known, number * UNIT + position, -1000.0)
+    unit_rows = lax.broadcasted_iota(jnp.int32, (NZ * UNIT, 2 * T), 0).astype(F32)
+    for half in range(2):
+        place[half] = jnp.where(unit_rows == back + half * SLOT, 1.0, 0.0).T.astype(BF)
+
+    def forward_unit(k):
+        rows = x[k].reshape(4 * UNIT, D)
         pre_g = jnp.dot(rows, wg[...], preferred_element_type=F32)
         pre_u = jnp.dot(rows, wu[...], preferred_element_type=F32)
         gh = lax.dot_general(rows, wd[...], NT_ROWS, preferred_element_type=F32)
-        a = pre_g.reshape(8, UNIT, F)[:, :SLOT]
-        u = pre_u.reshape(8, UNIT, F)[:, :SLOT]
-        h = gh.reshape(8, UNIT, F)[:, SLOT:]
+        a = pre_g.reshape(4, UNIT, F)[:, :SLOT]
+        u = pre_u.reshape(4, UNIT, F)[:, :SLOT]
+        h = gh.reshape(4, UNIT, F)[:, SLOT:]
         sigma = 1.0 / (1.0 + jnp.exp(-a))
         swish = a * sigma
         hidden = swish * u
         d_gate = h * u * sigma * (1.0 + a * (1.0 - sigma))
         d_up = h * swish
-        gall[g, 0, :, 0:F] = d_gate.reshape(192, F).astype(BF)
-        gall[g, 0, :, F : 2 * F] = d_up.reshape(192, F).astype(BF)
-        cols = pl.ds(pl.multiple_of(g * 384, 128), 384)
-        both = jnp.concatenate([jnp.zeros_like(hidden), hidden], axis=1).reshape(8 * UNIT, F)
-        at[:, cols] = both.T.astype(BF)
+        gall[k // 2, 0, k % 2, :, 0:F] = d_gate.reshape(96, F).astype(BF)
+        gall[k // 2, 0, k % 2, :, F : 2 * F] = d_up.reshape(96, F).astype(BF)
+        both = jnp.concatenate([jnp.zeros_like(hidden), hidden], axis=1)
+        hz[k] = both.reshape(4 * UNIT, F).astype(BF)
 
     def quarter(q):
         return pl.ds(pl.multiple_of(q * QUART, 128), QUART)
@@ -192,13 +201,17 @@
         src = xt.at[k, :, quarter(r)] if j == 0 else xq.at[k // 2, j, k % 2, 0]
         return rcopy(src, xq.at[k // 2, j, k % 2, 1], xc_s.at[k, j], xc_r.at[k, j], core_peer)
 
-    def g_send(g, j):
-        return rcopy(
-            gall.at[g, 0], gall.at[g, 4 - j], gs_s.at[g, j], gs_r.at[g, 4 - j], ((r + j) % 4, z, l)
-        )
-
-    def g_got(g, j):
-        return rcopy(gall.at[g, 0], gall.at[g, j], gs_s.at[g, j], gs_r.at[g, j], ((r + j) % 4, z, l))
+    def g_send(k, j):
+        return rcopy(
+            gall.at[k // 2, 0, k % 2], gall.at[k // 2, 4 - j, k % 2],
+            gs_s.at[k, j], gs_r.at[k, 4 - j], ((r + j) % 4, z, l),
+        )
+
+    def g_got(k, j):
+        return rcopy(
+            gall.at[k // 2, 0, k % 2], gall.at[k // 2, j, k % 2],
+            gs_s.at[k, j], gs_r.at[k, j], ((r + j) % 4, z, l),
+        )
 
     def compact(k):
         def columns(i, carry):
@@ -213,25 +226,20 @@
             xt_send(k, j).start()
         xq_fwd(k, 0).start()
 
-    def relay_quarters(g):
-        for kk in range(2):
-            for j in (1, 2, 3):
-                xt_got(2 * g + kk, j).wait_recv()
-                xq_fwd(2 * g + kk, j).start()
-
-    def send_grads(g):
-        for j in (2, 1, 3):
-            g_send(g, j).start()
+    def relay_quarters(k):
+        for j in (1, 2, 3):
+            xt_got(k, j).wait_recv()
+            xq_fwd(k, j).start()
 
     def accumulate(g, first):
         for kk in range(2):
             for j in range(4):
                 xq_fwd(2 * g + kk, j).wait_recv()
-        for j in (1, 2, 3):
-            g_got(g, j).wait_recv()
+            for j in (1, 2, 3):
+                g_got(2 * g + kk, j).wait_recv()
         rows = xq[g].reshape(4 * 192, QUART)
         for m in range(2):
-            left = gall[g, :, :, m * F : (m + 1) * F].reshape(4 * 192, F)
+            left = gall[g, :, :, :, m * F : (m + 1) * F].reshape(4 * 192, F)
             term = lax.dot_general(left, rows, (((0,), (0,)), ((), ())), preferred_element_type=F32)
             if first:
                 acc[m] = term
@@ -244,9 +252,9 @@
     def send_rb(k):
         return rcopy(part.at[k, 3], rdb.at[k], rb_s.at[k], rb_r.at[k], core_peer)
 
-    def route_group(g):
-        left = gall[g, 0, :, 0:F]
-        right = gall[g, 0, :, F : 2 * F]
+    def route_unit(k):
+        left = gall[k // 2, 0, k % 2, :, 0:F]
+        right = gall[k // 2, 0, k % 2, :, F : 2 * F]
 
         def columns(i, carry):
             done = []
@@ -254,16 +262,15 @@
                 cols = pl.ds(pl.multiple_of(half * HALF + i * 256, 256), 256)
                 one = lax.dot_general(left, wg[cols, :], NT_ROWS, preferred_element_type=F32)
                 one += lax.dot_general(right, wu[cols, :], NT_ROWS, preferred_element_type=F32)
-                done.append(one.reshape(2, 4, SLOT, 256))
-            part[pl.ds(2 * g, 2), :, :, pl.ds(pl.multiple_of(i * 256, 256), 256)] = (
-                jnp.concatenate(done, axis=2).astype(BF)
+                done.append(one.reshape(4, SLOT, 256))
+            part[k, :, :, pl.ds(pl.multiple_of(i * 256, 256), 256)] = (
+                jnp.concatenate(done, axis=1).astype(BF)
             )
             return carry
 
         lax.fori_loop(0, HALF // 256, columns, 0)
-        for kk in range(2):
-            send_ra(2 * g + kk).start()
-            send_rb(2 * g + kk).start()
+        send_rb(k).start()
+        send_ra(k).start()
 
     def y_return(k):
         return rcopy(part.at[k, 1], ry.at[k], ryy_s.at[k], ryy_r.at[k], y_peer)
@@ -284,57 +291,59 @@
         ).astype(BF)
         send_home(k).start()
 
+    def relay(k):
+        for h in range(2):
+            send_unit(k, h).wait_recv()
+            fwd_y(k, h).start()
+        fwd_d1(k).start()
+
     def turn(t, carry):
-        @pl.when(t < NZ)
-        def _():
-            send_unit(t).wait_recv()
-            fwd_y(t).start()
-            fwd_d1(t).start()
+        k = t - 1
+
+        @pl.when(t < NZ - 1)
+        def _():
+            relay(t)
 
         @pl.when(t > 0)
         def _():
-            k = t - 1
-            fwd_y(k).wait_recv()
+            fwd_y(k, 0).wait_recv()
+            fwd_y(k, 1).wait_recv()
             fwd_d2(k).start()
             compact(k)
-
-        even = t % 2 == 0
-
-        @pl.when(t == NZ)
-        def _():
+            fwd_d1(k).wait_recv()
+            fwd_d2(k).wait_recv()
+            forward_unit(k)
+            route_unit(k)
+            for j in (2, 1, 3):
+                g_send(k, j).start()
+
+        @pl.when((t > 0) & (t < NZ))
+        def _():
+            across(k)
+
+        @pl.when(t > 2)
+        def _():
+            relay_quarters(t - 3)
+
+        @pl.when(t == 5)
+        def _():
+            accumulate(0, True)
+
+        @pl.when(t == 7)
+        def _():
+            accumulate(1, False)
+            relay(7)
+
             def early(m, carry):
-                across(5 - m)
+                home(5 - m)
                 return carry
 
             lax.fori_loop(0, 6, early, 0)
 
-        @pl.when((t > 0) & even)
-        def _():
-            for kk in range(2):
-                fwd_d1(t - 2 + kk).wait_recv()
-                fwd_d2(t - 2 + kk).wait_recv()
-            forward_group(t // 2 - 1)
-
-        @pl.when((t > 0) & (t < NZ) & even)
-        def _():
-            send_grads(t // 2 - 1)
-            route_group(t // 2 - 1)
-
-        @pl.when((t > 3) & even)
-        def _():
-            relay_quarters(t // 2 - 2)
-
-        @pl.when(t == 6)
-        def _():
-            accumulate(0, True)
-
-        @pl.when(t == 8)
-        def _():
-            accumulate(1, False)
-
         return carry
 
     lax.fori_loop(0, NZ + 1, turn, 0)
+    at[...] = hz[...].reshape(32 * UNIT, F).T
 
     def weight_chunk(q):
         rows = x[:, :, :, quarter(q)].reshape(32 * UNIT, QUART)
@@ -352,13 +361,14 @@
     ]
 
     def step(j, carry):
-        weight_chunk((r + 2 + j + (j // 2)) % 4)
+        weight_chunk((r + (2 + j) * (j < 2) + (3 - j) * (j >= 2)) % 4)
 
         @pl.when(j == 0)
         def _():
             reduce[0].start()
             reduce[1].start()
-            send_grads(3)
+            across(7)
+            home(6)
 
         @pl.when(j == 1)
         def _():
@@ -370,23 +380,11 @@
 
         return carry
 
-    lax.fori_loop(0, 3, step, 0)
-    route_group(3)
-
-    def late(m, carry):
-        across(6 + m)
-        return carry
-
-    lax.fori_loop(0, 2, late, 0)
-
-    def first_home(m, carry):
-        home(5 - m)
-        return carry
-
-    lax.fori_loop(0, 3, first_home, 0)
-    weight_chunk(r)
-    relay_quarters(3)
+    lax.fori_loop(0, 4, step, 0)
     accumulate(2, False)
+    home(7)
+    relay_quarters(6)
+    relay_quarters(7)
 
     reduce[0].wait_recv()
     w[nxt, 0:128, :] = (w[nxt, 0:128, :].astype(F32) + ar[0].astype(F32)).astype(BF)
@@ -394,14 +392,9 @@
     reduce[1].wait_recv()
     w[prv, 128:256, :] = (w[prv, 128:256, :].astype(F32) + ar[1].astype(F32)).astype(BF)
     reduce[5].start()
-
-    def second_home(m, carry):
-        home((m < 3) * (2 - m) + (m >= 3) * (m + 3))
-        return carry
-
-    lax.fori_loop(0, 5, second_home, 0)
     accumulate(3, False)
-    gw_ref[0 : 2 * F, :] = acc[...].reshape(2 * F, QUART).astype(BF)
+    gg_ref[...] = acc[0].T.astype(BF)
+    gu_ref[...] = acc[1].T.astype(BF)
 
     def arrived(j, carry):
         rcopy(part.at[j, 0], ret.at[j], h_s.at[j], h_r.at[j], source(0)).wait_recv()
@@ -409,39 +402,45 @@
 
     lax.fori_loop(0, NZ, arrived, 0)
 
-    unit_rows = lax.broadcasted_iota(jnp.int32, (NZ * UNIT, 2 * T), 0).astype(F32)
-
-    def last(i, carry):
-        cols = pl.ds(pl.multiple_of(i * 256, 256), 256)
-        rows = ret[:, :, cols].reshape(NZ * UNIT, 256)
-        for half in range(2):
-            pick_t = jnp.where(unit_rows == place[0:1, :] + half * SLOT, 1.0, 0.0).astype(BF)
-            got = lax.dot_general(
-                pick_t, rows, (((0,), (0,)), ((), ())), preferred_element_type=F32
-            )
-            both = got.reshape(2, T, 256).astype(BF)
+    def final(half):
+        cols = pl.ds(half * HALF, HALF)
+        return rcopy(
+            fin_send.at[1 - c, :, cols], fin_recv.at[:, cols], f_s.at[half], f_r.at[half], core_peer
+        )
+
+    for half in range(2):
+
+        def last(i, carry):
+            cols = pl.ds(pl.multiple_of(i * 256, 256), 256)
+            rows = ret[:, :, cols].reshape(NZ * UNIT, 256)
+            got = jnp.dot(place[half], rows, preferred_element_type=F32)
             outc = pl.ds(pl.multiple_of(half * HALF + i * 256, 256), 256)
-            fin_send[:, :, outc] = both
-        return carry
-
-    lax.fori_loop(0, HALF // 256, last, 0)
-    final = rcopy(fin_send.at[1 - c], fin_recv, f_s, f_r, core_peer)
-    final.start()
-    final.wait_recv()
-    gt_ref[...] = (fin_send[c].astype(F32) + fin_recv[...].astype(F32)).astype(BF)
+            fin_send[:, :, outc] = got.reshape(2, T, 256).astype(BF)
+            return carry
+
+        lax.fori_loop(0, HALF // 256, last, 0)
+        final(half).start()
 
     for j in (2, 3, 4, 5):
         reduce[j].wait_recv()
-    gw_ref[2 * F :, :] = (
+    gd_ref[...] = (
         w[r].astype(F32) + br[0].astype(F32) + br[1].astype(F32)
     ).astype(BF)
 
-    for copy in exchange + reduce + [final]:
+    for half in range(2):
+        final(half).wait_recv()
+        cols = slice(half * HALF, (half + 1) * HALF)
+        gt_ref[:, cols] = (
+            fin_send[c, :, cols].astype(F32) + fin_recv[:, cols].astype(F32)
+        ).astype(BF)
+
+    for copy in exchange + reduce + [final(0), final(1)]:
         copy.wait_send()
 
     def drain(k, carry):
-        send_unit(k).wait_send()
-        fwd_y(k).wait_send()
+        for h in range(2):
+            send_unit(k, h).wait_send()
+            fwd_y(k, h).wait_send()
         fwd_d1(k).wait_send()
         fwd_d2(k).wait_send()
         send_ra(k).wait_send()
@@ -452,12 +451,10 @@
             xq_fwd(k, j).wait_send()
         for j in (1, 2, 3):
             xt_send(k, j).wait_send()
+            g_send(k, j).wait_send()
         return carry
 
     lax.fori_loop(0, NZ, drain, 0)
-    for g in range(4):
-        for j in (1, 2, 3):
-            g_send(g, j).wait_send()
 
 
 def on_device(tokens, grad_out, gates, routes, w_gate, w_up, w_down):
@@ -465,14 +462,16 @@
     vmem = pl.BlockSpec(memory_space=pltpu.VMEM)
     anyspace = pl.BlockSpec(memory_space=pl.ANY)
     flops = 2 * 1536 * D * F * 7
-    grad_tokens, grads = pl.pallas_call(
+    grad_tokens, grad_gate, grad_up, grad_down = pl.pallas_call(
         kernel,
         out_shape=(
             jax.ShapeDtypeStruct((T, D), BF),
-            jax.ShapeDtypeStruct((3 * F, QUART), BF),
+            jax.ShapeDtypeStruct((QUART, F), BF),
+            jax.ShapeDtypeStruct((QUART, F), BF),
+            jax.ShapeDtypeStruct((F, QUART), BF),
         ),
         in_specs=[anyspace, anyspace, vmem, vmem, anyspace, anyspace, anyspace],
-        out_specs=(vmem, vmem),
+        out_specs=(vmem, vmem, vmem, vmem),
         scratch_shapes=[
             pltpu.VMEM((4 * T, D), BF),
             pltpu.VMEM((2, 8, T), F32),
@@ -492,18 +491,19 @@
             pltpu.VMEM((2, F, QUART), BF),
             pltpu.VMEM((2, T, D), BF),
             pltpu.VMEM((T, D), BF),
-            pltpu.VMEM((8, 2 * T), F32),
+            pltpu.VMEM((2, 2 * T, NZ * UNIT), BF),
             pltpu.VMEM((NZ, UNIT, D), BF),
             pltpu.VMEM((4, 4, 2, 2, UNIT, QUART), BF),
-            pltpu.VMEM((4, 4, 192, 2 * F), BF),
+            pltpu.VMEM((4, 4, 2, 96, 2 * F), BF),
             pltpu.VMEM((2, F, QUART), F32),
+            pltpu.VMEM((NZ, 4 * UNIT, F), BF),
             dma((5,)), dma((3,)), dma((3,)),
+            dma((NZ, 2)), dma((NZ, 2)), dma((NZ, 2)), dma((NZ, 2)),
             dma((NZ,)), dma((NZ,)), dma((NZ,)), dma((NZ,)),
             dma((NZ,)), dma((NZ,)), dma((NZ,)), dma((NZ,)),
             dma((NZ,)), dma((NZ,)), dma((NZ,)), dma((NZ,)),
-            dma((NZ,)), dma((NZ,)), dma((NZ,)), dma((NZ,)),
-            dma((6,)), dma((6,)), dma, dma,
-            dma((NZ, 4)), dma((NZ, 4)), dma((NZ, 4)), dma((NZ, 4)), dma((4, 4)), dma((4, 4)),
+            dma((6,)), dma((6,)), dma((2,)), dma((2,)),
+            dma((NZ, 4)), dma((NZ, 4)), dma((NZ, 4)), dma((NZ, 4)), dma((NZ, 4)), dma((NZ, 4)),
         ],
         compiler_params=pltpu.CompilerParams(
             collective_id=0, has_side_effects=True, vmem_limit_bytes=62 * 1024 * 1024
@@ -513,12 +513,7 @@
         tokens, grad_out, gates.reshape(1, T), routes.reshape(1, T),
         w_gate[0], w_up[0], w_down[0],
     )
-    return (
-        grad_tokens,
-        grads[:F].T[None],
-        grads[F : 2 * F].T[None],
-        grads[2 * F :][None],
-    )
+    return (grad_tokens, grad_gate[None], grad_up[None], grad_down[None])
 
 
 def solution(mesh):

time: 157 us -> 161 us (1.025); the launches traced: 157 us -> 158 us
  Pallas kernels: 151 us -> 153 us
    broadcast_in_dim x1 -> x0, local copies, waits for them, and re-layouts: 2.25 us -> none  [on_device(): grads[2 * F:][None]]
    pallas_call x1, Pallas kernels: 151 us -> 153 us  [on_device(): pl.pallas_call(kernel, out_shape=(jax.ShapeDtypeStruct((T, D), BF), jax.S...]
    unnamed x5 -> x10, local copies, waits for them, and re-layouts: 2.89 us -> 4.58 us
where the time goes in v3:
time: 161 us; the launch traced here: 158 us
  Pallas kernels  153 us (95%)
  local copies, waits for them, and re-layouts  4.58 us (3%)
    pallas_call x1, Pallas kernels, on_device(): pl.pallas_call(kernel, out_shape=(jax.ShapeDtypeStruct((T, D), BF), jax.S...  153 us
    unnamed x10, local copies, waits for them, and re-layouts  4.58 us

profile of v3, /device:TPU:1, one launch (start us, length us, event | category | flops | bytes accessed | tf_op | source)
XLA Modules:
  0.0 158.3 jit_solution(17647249409412146733)
XLA Ops:
  0.6 153.1 %shard_map.102 = (bf16[128,3584]{1,0:T(8,128)(2,1)}, bf16[896,256]{1,0:T(8,128)(2,1)}, bf16[896,256]{1,0:T(8,128)(2,1)}, bf16[256,896]{1,0:T(8,128)(2,1)}) custom-call(bf16[128,3584]{1,0:T(8,128)(2,1)} %tok_hbm.1, bf16[128,3584]{1,0:T(8,128)(2,1)} %grad_hbm.1, f32[1,128]{1,0:T(1,128)} %bitcast.14, s32[1,128]{1,0:T(1,128)} %bitcast.15, ...), custom_call_target="tpu_custom_call" | custom-call | flops 19730006016 | bytes 10000000 | tf_op jit(solution)/shard_map/pallas_call | solution.py:465
  153.7 0.0 copy-start.2
  153.7 0.0 copy-start.1
  153.7 0.0 copy-start
  153.8 2.3 %copy.15 = bf16[128,3584]{1,0:T(8,128)(2,1)} copy(bf16[128,3584]{1,0:T(8,128)(2,1)} %get-tuple-element.16) | data formatting | bytes 1835008
  156.0 0.0 copy-done.2
  156.0 0.8 copy.16
  156.8 0.0 copy-done.1
  156.8 0.8 copy.17
  157.6 0.0 copy-done
  157.6 0.8 copy.18
Async XLA Ops:
  153.7 2.3 %copy-start.2 = (bf16[896,256]{1,0:T(8,128)(2,1)S(1)}, bf16[896,256]{1,0:T(8,128)(2,1)}, u32[]{:S(2)}) copy-start(bf16[896,256]{1,0:T(8,128)(2,1)} %get-tuple-element.9) | copy-start | bytes 1376260
  153.7 3.1 %copy-start.1 = (bf16[896,256]{1,0:T(8,128)(2,1)S(1)}, bf16[896,256]{1,0:T(8,128)(2,1)}, u32[]{:S(2)}) copy-start(bf16[896,256]{1,0:T(8,128)(2,1)} %get-tuple-element.10) | copy-start | bytes 1376260
  153.7 3.8 %copy-start = (bf16[256,896]{1,0:T(8,128)(2,1)S(1)}, bf16[256,896]{1,0:T(8,128)(2,1)}, u32[]{:S(2)}) copy-start(bf16[256,896]{1,0:T(8,128)(2,1)} %get-tuple-element.11) | copy-start | bytes 1376260

commit v4 on v3

--- a/solution.py
+++ b/solution.py
@@ -164,23 +164,25 @@
     for half in range(2):
         place[half] = jnp.where(unit_rows == back + half * SLOT, 1.0, 0.0).T.astype(BF)
 
-    def forward_unit(k):
-        rows = x[k].reshape(4 * UNIT, D)
+    def forward_units(k, n):
+        these = pl.ds(k, n)
+        rows = x[these].reshape(n * 4 * UNIT, D)
         pre_g = jnp.dot(rows, wg[...], preferred_element_type=F32)
         pre_u = jnp.dot(rows, wu[...], preferred_element_type=F32)
         gh = lax.dot_general(rows, wd[...], NT_ROWS, preferred_element_type=F32)
-        a = pre_g.reshape(4, UNIT, F)[:, :SLOT]
-        u = pre_u.reshape(4, UNIT, F)[:, :SLOT]
-        h = gh.reshape(4, UNIT, F)[:, SLOT:]
+        a = pre_g.reshape(n * 4, UNIT, F)[:, :SLOT]
+        u = pre_u.reshape(n * 4, UNIT, F)[:, :SLOT]
+        h = gh.reshape(n * 4, UNIT, F)[:, SLOT:]
         sigma = 1.0 / (1.0 + jnp.exp(-a))
         swish = a * sigma
         hidden = swish * u
         d_gate = h * u * sigma * (1.0 + a * (1.0 - sigma))
         d_up = h * swish
-        gall[k // 2, 0, k % 2, :, 0:F] = d_gate.reshape(96, F).astype(BF)
-        gall[k // 2, 0, k % 2, :, F : 2 * F] = d_up.reshape(96, F).astype(BF)
+        place_g = pl.ds(k % 2, n)
+        gall[k // 2, 0, place_g, :, 0:F] = d_gate.reshape(n, 96, F).astype(BF)
+        gall[k // 2, 0, place_g, :, F : 2 * F] = d_up.reshape(n, 96, F).astype(BF)
         both = jnp.concatenate([jnp.zeros_like(hidden), hidden], axis=1)
-        hz[k] = both.reshape(4 * UNIT, F).astype(BF)
+        hz[these] = both.reshape(n, 4 * UNIT, F).astype(BF)
 
     def quarter(q):
         return pl.ds(pl.multiple_of(q * QUART, 128), QUART)
@@ -252,9 +254,9 @@
     def send_rb(k):
         return rcopy(part.at[k, 3], rdb.at[k], rb_s.at[k], rb_r.at[k], core_peer)
 
-    def route_unit(k):
-        left = gall[k // 2, 0, k % 2, :, 0:F]
-        right = gall[k // 2, 0, k % 2, :, F : 2 * F]
+    def route_units(k, n):
+        left = gall[k // 2, 0, pl.ds(k % 2, n), :, 0:F].reshape(n * 96, F)
+        right = gall[k // 2, 0, pl.ds(k % 2, n), :, F : 2 * F].reshape(n * 96, F)
 
         def columns(i, carry):
             done = []
@@ -262,15 +264,18 @@
                 cols = pl.ds(pl.multiple_of(half * HALF + i * 256, 256), 256)
                 one = lax.dot_general(left, wg[cols, :], NT_ROWS, preferred_element_type=F32)
                 one += lax.dot_general(right, wu[cols, :], NT_ROWS, preferred_element_type=F32)
-                done.append(one.reshape(4, SLOT, 256))
-            part[k, :, :, pl.ds(pl.multiple_of(i * 256, 256), 256)] = (
-                jnp.concatenate(done, axis=1).astype(BF)
+                done.append(one.reshape(n, 4, SLOT, 256))
+            part[pl.ds(k, n), :, :, pl.ds(pl.multiple_of(i * 256, 256), 256)] = (
+                jnp.concatenate(done, axis=2).astype(BF)
             )
             return carry
 
         lax.fori_loop(0, HALF // 256, columns, 0)
-        send_rb(k).start()
-        send_ra(k).start()
+        for i in range(n):
+            send_rb(k + i).start()
+            send_ra(k + i).start()
+            for j in (2, 1, 3):
+                g_send(k + i, j).start()
 
     def y_return(k):
         return rcopy(part.at[k, 1], ry.at[k], ryy_s.at[k], ryy_r.at[k], y_peer)
@@ -310,16 +315,27 @@
             fwd_y(k, 1).wait_recv()
             fwd_d2(k).start()
             compact(k)
+
+        @pl.when((t > 0) & (t < NZ - 1) & (t % 2 == 0))
+        def _():
+            for i in range(2):
+                fwd_d1(t - 2 + i).wait_recv()
+                fwd_d2(t - 2 + i).wait_recv()
+            forward_units(t - 2, 2)
+            route_units(t - 2, 2)
+            across(t - 2)
+            across(t - 1)
+
+        @pl.when(t >= NZ - 1)
+        def _():
             fwd_d1(k).wait_recv()
             fwd_d2(k).wait_recv()
-            forward_unit(k)
-            route_unit(k)
-            for j in (2, 1, 3):
-                g_send(k, j).start()
-
-        @pl.when((t > 0) & (t < NZ))
-        def _():
-            across(k)
+            forward_units(k, 1)
+            route_units(k, 1)
+
+        @pl.when(t == NZ - 1)
+        def _():
+            across(NZ - 2)
 
         @pl.when(t > 2)
         def _():

time: 161 us -> 161 us (level)
  no operation moved by 1% of the time
where the time goes in v4:
time: 161 us; the launch traced here: 159 us
  Pallas kernels  154 us (96%)
  local copies, waits for them, and re-layouts  4.58 us (3%)
    pallas_call x1, Pallas kernels, on_device(): pl.pallas_call(kernel, out_shape=(jax.ShapeDtypeStruct((T, D), BF), jax.S...  154 us
    unnamed x10, local copies, waits for them, and re-layouts  4.58 us

profile of v4, /device:TPU:1, one launch (start us, length us, event | category | flops | bytes accessed | tf_op | source)
XLA Modules:
  0.0 159.2 jit_solution(10376358770144131383)
XLA Ops:
  0.6 153.9 %shard_map.102 = (bf16[128,3584]{1,0:T(8,128)(2,1)}, bf16[896,256]{1,0:T(8,128)(2,1)}, bf16[896,256]{1,0:T(8,128)(2,1)}, bf16[256,896]{1,0:T(8,128)(2,1)}) custom-call(bf16[128,3584]{1,0:T(8,128)(2,1)} %tok_hbm.1, bf16[128,3584]{1,0:T(8,128)(2,1)} %grad_hbm.1, f32[1,128]{1,0:T(1,128)} %bitcast.14, s32[1,128]{1,0:T(1,128)} %bitcast.15, ...), custom_call_target="tpu_custom_call" | custom-call | flops 19730006016 | bytes 10000000 | tf_op jit(solution)/shard_map/pallas_call | solution.py:481
  154.6 0.0 copy-start.2
  154.6 0.0 copy-start.1
  154.6 0.0 copy-start
  154.6 2.3 %copy.15 = bf16[128,3584]{1,0:T(8,128)(2,1)} copy(bf16[128,3584]{1,0:T(8,128)(2,1)} %get-tuple-element.16) | data formatting | bytes 1835008
  156.9 0.0 copy-done.2
  156.9 0.8 copy.16
  157.6 0.0 copy-done.1
  157.6 0.8 copy.17
  158.4 0.0 copy-done
  158.4 0.8 copy.18
Async XLA Ops:
  154.6 2.3 %copy-start.2 = (bf16[896,256]{1,0:T(8,128)(2,1)S(1)}, bf16[896,256]{1,0:T(8,128)(2,1)}, u32[]{:S(2)}) copy-start(bf16[896,256]{1,0:T(8,128)(2,1)} %get-tuple-element.9) | copy-start | bytes 1376260
  154.6 3.1 %copy-start.1 = (bf16[896,256]{1,0:T(8,128)(2,1)S(1)}, bf16[896,256]{1,0:T(8,128)(2,1)}, u32[]{:S(2)}) copy-start(bf16[896,256]{1,0:T(8,128)(2,1)} %get-tuple-element.10) | copy-start | bytes 1376260
  154.6 3.8 %copy-start = (bf16[256,896]{1,0:T(8,128)(2,1)S(1)}, bf16[256,896]{1,0:T(8,128)(2,1)}, u32[]{:S(2)}) copy-start(bf16[256,896]{1,0:T(8,128)(2,1)} %get-tuple-element.11) | copy-start | bytes 1376260

commit v5 on v3

--- a/solution.py
+++ b/solution.py
@@ -28,7 +28,7 @@
     tok_hbm, grad_hbm, gate_ref, route_ref, wg_hbm, wu_hbm, wd_hbm,
     gt_ref, gg_ref, gu_ref, gd_ref,
     stage, meta, out, x, wg, wu, wd, at, part, rda, rdb, ry, ret, w, ar, br, fin_send, fin_recv, place,
-    xt, xq, gall, acc, hz,
+    xt, xq, gall, acc,
     loc, ex_s, ex_r, z_s, z_r, y_s, y_r, d1_s, d1_r, d2_s, d2_r,
     ra_s, ra_r, rb_s, rb_r, ryy_s, ryy_r, h_s, h_r, rs_s, rs_r, f_s, f_r,
     xs_s, xs_r, xc_s, xc_r, gs_s, gs_r,
@@ -164,23 +164,25 @@
     for half in range(2):
         place[half] = jnp.where(unit_rows == back + half * SLOT, 1.0, 0.0).T.astype(BF)
 
-    def forward_unit(k):
-        rows = x[k].reshape(4 * UNIT, D)
+    def forward_group(g):
+        units = x.at[pl.ds(2 * g, 2)]
+        rows = units[...].reshape(8 * UNIT, D)
         pre_g = jnp.dot(rows, wg[...], preferred_element_type=F32)
         pre_u = jnp.dot(rows, wu[...], preferred_element_type=F32)
         gh = lax.dot_general(rows, wd[...], NT_ROWS, preferred_element_type=F32)
-        a = pre_g.reshape(4, UNIT, F)[:, :SLOT]
-        u = pre_u.reshape(4, UNIT, F)[:, :SLOT]
-        h = gh.reshape(4, UNIT, F)[:, SLOT:]
+        a = pre_g.reshape(8, UNIT, F)[:, :SLOT]
+        u = pre_u.reshape(8, UNIT, F)[:, :SLOT]
+        h = gh.reshape(8, UNIT, F)[:, SLOT:]
         sigma = 1.0 / (1.0 + jnp.exp(-a))
         swish = a * sigma
         hidden = swish * u
         d_gate = h * u * sigma * (1.0 + a * (1.0 - sigma))
         d_up = h * swish
-        gall[k // 2, 0, k % 2, :, 0:F] = d_gate.reshape(96, F).astype(BF)
-        gall[k // 2, 0, k % 2, :, F : 2 * F] = d_up.reshape(96, F).astype(BF)
-        both = jnp.concatenate([jnp.zeros_like(hidden), hidden], axis=1)
-        hz[k] = both.reshape(4 * UNIT, F).astype(BF)
+        gall[g, 0, :, 0:F] = d_gate.reshape(192, F).astype(BF)
+        gall[g, 0, :, F : 2 * F] = d_up.reshape(192, F).astype(BF)
+        cols = pl.ds(pl.multiple_of(g * 384, 128), 384)
+        both = jnp.concatenate([jnp.zeros_like(hidden), hidden], axis=1).reshape(8 * UNIT, F)
+        at[:, cols] = both.T.astype(BF)
 
     def quarter(q):
         return pl.ds(pl.multiple_of(q * QUART, 128), QUART)
@@ -201,17 +203,13 @@
         src = xt.at[k, :, quarter(r)] if j == 0 else xq.at[k // 2, j, k % 2, 0]
         return rcopy(src, xq.at[k // 2, j, k % 2, 1], xc_s.at[k, j], xc_r.at[k, j], core_peer)
 
-    def g_send(k, j):
+    def g_send(g, j):
         return rcopy(
-            gall.at[k // 2, 0, k % 2], gall.at[k // 2, 4 - j, k % 2],
-            gs_s.at[k, j], gs_r.at[k, 4 - j], ((r + j) % 4, z, l),
-        )
-
-    def g_got(k, j):
-        return rcopy(
-            gall.at[k // 2, 0, k % 2], gall.at[k // 2, j, k % 2],
-            gs_s.at[k, j], gs_r.at[k, j], ((r + j) % 4, z, l),
-        )
+            gall.at[g, 0], gall.at[g, 4 - j], gs_s.at[g, j], gs_r.at[g, 4 - j], ((r + j) % 4, z, l)
+        )
+
+    def g_got(g, j):
+        return rcopy(gall.at[g, 0], gall.at[g, j], gs_s.at[g, j], gs_r.at[g, j], ((r + j) % 4, z, l))
 
     def compact(k):
         def columns(i, carry):
@@ -226,20 +224,25 @@
             xt_send(k, j).start()
         xq_fwd(k, 0).start()
 
-    def relay_quarters(k):
-        for j in (1, 2, 3):
-            xt_got(k, j).wait_recv()
-            xq_fwd(k, j).start()
+    def relay_quarters(g):
+        for kk in range(2):
+            for j in (1, 2, 3):
+                xt_got(2 * g + kk, j).wait_recv()
+                xq_fwd(2 * g + kk, j).start()
+
+    def send_grads(g):
+        for j in (2, 1, 3):
+            g_send(g, j).start()
 
     def accumulate(g, first):
         for kk in range(2):
             for j in range(4):
                 xq_fwd(2 * g + kk, j).wait_recv()
-            for j in (1, 2, 3):
-                g_got(2 * g + kk, j).wait_recv()
+        for j in (1, 2, 3):
+            g_got(g, j).wait_recv()
         rows = xq[g].reshape(4 * 192, QUART)
         for m in range(2):
-            left = gall[g, :, :, :, m * F : (m + 1) * F].reshape(4 * 192, F)
+            left = gall[g, :, :, m * F : (m + 1) * F].reshape(4 * 192, F)
             term = lax.dot_general(left, rows, (((0,), (0,)), ((), ())), preferred_element_type=F32)
             if first:
                 acc[m] = term
@@ -252,9 +255,9 @@
     def send_rb(k):
         return rcopy(part.at[k, 3], rdb.at[k], rb_s.at[k], rb_r.at[k], core_peer)
 
-    def route_unit(k):
-        left = gall[k // 2, 0, k % 2, :, 0:F]
-        right = gall[k // 2, 0, k % 2, :, F : 2 * F]
+    def route_group(g):
+        left = gall[g, 0, :, 0:F]
+        right = gall[g, 0, :, F : 2 * F]
 
         def columns(i, carry):
             done = []
@@ -262,15 +265,16 @@
                 cols = pl.ds(pl.multiple_of(half * HALF + i * 256, 256), 256)
                 one = lax.dot_general(left, wg[cols, :], NT_ROWS, preferred_element_type=F32)
                 one += lax.dot_general(right, wu[cols, :], NT_ROWS, preferred_element_type=F32)
-                done.append(one.reshape(4, SLOT, 256))
-            part[k, :, :, pl.ds(pl.multiple_of(i * 256, 256), 256)] = (
-                jnp.concatenate(done, axis=1).astype(BF)
+                done.append(one.reshape(2, 4, SLOT, 256))
+            part[pl.ds(2 * g, 2), :, :, pl.ds(pl.multiple_of(i * 256, 256), 256)] = (
+                jnp.concatenate(done, axis=2).astype(BF)
             )
             return carry
 
         lax.fori_loop(0, HALF // 256, columns, 0)
-        send_rb(k).start()
-        send_ra(k).start()
+        for kk in range(2):
+            send_ra(2 * g + kk).start()
+            send_rb(2 * g + kk).start()
 
     def y_return(k):
         return rcopy(part.at[k, 1], ry.at[k], ryy_s.at[k], ryy_r.at[k], y_peer)
@@ -291,39 +295,44 @@
         ).astype(BF)
         send_home(k).start()
 
-    def relay(k):
-        for h in range(2):
-            send_unit(k, h).wait_recv()
-            fwd_y(k, h).start()
-        fwd_d1(k).start()
-
     def turn(t, carry):
-        k = t - 1
-
-        @pl.when(t < NZ - 1)
-        def _():
-            relay(t)
+        @pl.when(t < NZ)
+        def _():
+            for h in range(2):
+                send_unit(t, h).wait_recv()
+                fwd_y(t, h).start()
+            fwd_d1(t).start()
 
         @pl.when(t > 0)
         def _():
-            fwd_y(k, 0).wait_recv()
-            fwd_y(k, 1).wait_recv()
-            fwd_d2(k).start()
-            compact(k)
-            fwd_d1(k).wait_recv()
-            fwd_d2(k).wait_recv()
-            forward_unit(k)
-            route_unit(k)
-            for j in (2, 1, 3):
-                g_send(k, j).start()
-
-        @pl.when((t > 0) & (t < NZ))
-        def _():
-            across(k)
-
-        @pl.when(t > 2)
-        def _():
-            relay_quarters(t - 3)
+            fwd_y(t - 1, 0).wait_recv()
+            fwd_y(t - 1, 1).wait_recv()
+            fwd_d2(t - 1).start()
+            compact(t - 1)
+
+        even = t % 2 == 0
+
+        @pl.when(t == NZ)
+        def _():
+            across(5)
+            across(4)
+            across(3)
+
+        @pl.when((t > 0) & even)
+        def _():
+            for kk in range(2):
+                fwd_d1(t - 2 + kk).wait_recv()
+                fwd_d2(t - 2 + kk).wait_recv()
+            forward_group(t // 2 - 1)
+            route_group(t // 2 - 1)
+
+        @pl.when((t > 0) & (t < NZ) & even)
+        def _():
+            send_grads(t // 2 - 1)
+
+        @pl.when((t > 2) & (t % 2 == 1))
+        def _():
+            relay_quarters((t - 3) // 2)
 
         @pl.when(t == 5)
         def _():
@@ -332,18 +341,10 @@
         @pl.when(t == 7)
         def _():
             accumulate(1, False)
-            relay(7)
-
-            def early(m, carry):
-                home(5 - m)
-                return carry
-
-            lax.fori_loop(0, 6, early, 0)
 
         return carry
 
     lax.fori_loop(0, NZ + 1, turn, 0)
-    at[...] = hz[...].reshape(32 * UNIT, F).T
 
     def weight_chunk(q):
         rows = x[:, :, :, quarter(q)].reshape(32 * UNIT, QUART)
@@ -367,24 +368,32 @@
         def _():
             reduce[0].start()
             reduce[1].start()
-            across(7)
-            home(6)
+            send_grads(3)
+
+            def rest(m, carry):
+                across((6 + m) * (m < 2) + (4 - m) * (m >= 2))
+                return carry
+
+            lax.fori_loop(0, 5, rest, 0)
+            home(5)
 
         @pl.when(j == 1)
         def _():
             reduce[3].start()
+            home(4)
 
         @pl.when(j == 2)
         def _():
             reduce[2].start()
+            home(3)
 
         return carry
 
     lax.fori_loop(0, 4, step, 0)
     accumulate(2, False)
+    home(6)
     home(7)
-    relay_quarters(6)
-    relay_quarters(7)
+    relay_quarters(3)
 
     reduce[0].wait_recv()
     w[nxt, 0:128, :] = (w[nxt, 0:128, :].astype(F32) + ar[0].astype(F32)).astype(BF)
@@ -392,6 +401,12 @@
     reduce[1].wait_recv()
     w[prv, 128:256, :] = (w[prv, 128:256, :].astype(F32) + ar[1].astype(F32)).astype(BF)
     reduce[5].start()
+
+    def near_home(m, carry):
+        home(2 - m)
+        return carry
+
+    lax.fori_loop(0, 3, near_home, 0)
     accumulate(3, False)
     gg_ref[...] = acc[0].T.astype(BF)
     gu_ref[...] = acc[1].T.astype(BF)
@@ -451,10 +466,12 @@
             xq_fwd(k, j).wait_send()
         for j in (1, 2, 3):
             xt_send(k, j).wait_send()
-            g_send(k, j).wait_send()
         return carry
 
     lax.fori_loop(0, NZ, drain, 0)
+    for g in range(4):
+        for j in (1, 2, 3):
+            g_send(g, j).wait_send()
 
 
 def on_device(tokens, grad_out, gates, routes, w_gate, w_up, w_down):
@@ -494,16 +511,15 @@
             pltpu.VMEM((2, 2 * T, NZ * UNIT), BF),
             pltpu.VMEM((NZ, UNIT, D), BF),
             pltpu.VMEM((4, 4, 2, 2, UNIT, QUART), BF),
-            pltpu.VMEM((4, 4, 2, 96, 2 * F), BF),
+            pltpu.VMEM((4, 4, 192, 2 * F), BF),
             pltpu.VMEM((2, F, QUART), F32),
-            pltpu.VMEM((NZ, 4 * UNIT, F), BF),
             dma((5,)), dma((3,)), dma((3,)),
             dma((NZ, 2)), dma((NZ, 2)), dma((NZ, 2)), dma((NZ, 2)),
             dma((NZ,)), dma((NZ,)), dma((NZ,)), dma((NZ,)),
             dma((NZ,)), dma((NZ,)), dma((NZ,)), dma((NZ,)),
             dma((NZ,)), dma((NZ,)), dma((NZ,)), dma((NZ,)),
             dma((6,)), dma((6,)), dma((2,)), dma((2,)),
-            dma((NZ, 4)), dma((NZ, 4)), dma((NZ, 4)), dma((NZ, 4)), dma((NZ, 4)), dma((NZ, 4)),
+            dma((NZ, 4)), dma((NZ, 4)), dma((NZ, 4)), dma((NZ, 4)), dma((4, 4)), dma((4, 4)),
         ],
         compiler_params=pltpu.CompilerParams(
             collective_id=0, has_side_effects=True, vmem_limit_bytes=62 * 1024 * 1024

time: 161 us -> 149 us (0.925)
  Pallas kernels: 153 us -> 141 us
    pallas_call x1, Pallas kernels: 153 us -> 141 us  [on_device(): pl.pallas_call(kernel, out_shape=(jax.ShapeDtypeStruct((T, D), BF), jax.S...]
where the time goes in v5:
time: 149 us; the launch traced here: 146 us
  Pallas kernels  141 us (95%)
  local copies, waits for them, and re-layouts  4.58 us (3%)
    pallas_call x1, Pallas kernels, on_device(): pl.pallas_call(kernel, out_shape=(jax.ShapeDtypeStruct((T, D), BF), jax.S...  141 us
    unnamed x10, local copies, waits for them, and re-layouts  4.58 us

profile of v5, /device:TPU:1, one launch (start us, length us, event | category | flops | bytes accessed | tf_op | source)
XLA Modules:
  0.0 146.1 jit_solution(9626750840183929731)
XLA Ops:
  0.6 140.9 %shard_map.102 = (bf16[128,3584]{1,0:T(8,128)(2,1)}, bf16[896,256]{1,0:T(8,128)(2,1)}, bf16[896,256]{1,0:T(8,128)(2,1)}, bf16[256,896]{1,0:T(8,128)(2,1)}) custom-call(bf16[128,3584]{1,0:T(8,128)(2,1)} %tok_hbm.1, bf16[128,3584]{1,0:T(8,128)(2,1)} %grad_hbm.1, f32[1,128]{1,0:T(1,128)} %bitcast.14, s32[1,128]{1,0:T(1,128)} %bitcast.15, ...), custom_call_target="tpu_custom_call" | custom-call | flops 19730006016 | bytes 10000000 | tf_op jit(solution)/shard_map/pallas_call | solution.py:482
  141.5 0.0 copy-start.2
  141.5 0.0 copy-start.1
  141.5 0.0 copy-start
  141.5 2.3 %copy.15 = bf16[128,3584]{1,0:T(8,128)(2,1)} copy(bf16[128,3584]{1,0:T(8,128)(2,1)} %get-tuple-element.16) | data formatting | bytes 1835008
  143.8 0.0 copy-done.2
  143.8 0.8 copy.16
  144.6 0.0 copy-done.1
  144.6 0.8 copy.17
  145.4 0.0 copy-done
  145.4 0.8 copy.18
Async XLA Ops:
  141.5 2.3 %copy-start.2 = (bf16[896,256]{1,0:T(8,128)(2,1)S(1)}, bf16[896,256]{1,0:T(8,128)(2,1)}, u32[]{:S(2)}) copy-start(bf16[896,256]{1,0:T(8,128)(2,1)} %get-tuple-element.9) | copy-start | bytes 1376260
  141.5 3.1 %copy-start.1 = (bf16[896,256]{1,0:T(8,128)(2,1)S(1)}, bf16[896,256]{1,0:T(8,128)(2,1)}, u32[]{:S(2)}) copy-start(bf16[896,256]{1,0:T(8,128)(2,1)} %get-tuple-element.10) | copy-start | bytes 1376260
  141.5 3.8 %copy-start = (bf16[256,896]{1,0:T(8,128)(2,1)S(1)}, bf16[256,896]{1,0:T(8,128)(2,1)}, u32[]{:S(2)}) copy-start(bf16[256,896]{1,0:T(8,128)(2,1)} %get-tuple-element.11) | copy-start | bytes 1376260

commit v6 on v5

--- a/solution.py
+++ b/solution.py
@@ -295,13 +295,16 @@
         ).astype(BF)
         send_home(k).start()
 
+    def relay(k):
+        for h in range(2):
+            send_unit(k, h).wait_recv()
+            fwd_y(k, h).start()
+        fwd_d1(k).start()
+
     def turn(t, carry):
-        @pl.when(t < NZ)
-        def _():
-            for h in range(2):
-                send_unit(t, h).wait_recv()
-                fwd_y(t, h).start()
-            fwd_d1(t).start()
+        @pl.when(t < NZ - 1)
+        def _():
+            relay(t)
 
         @pl.when(t > 0)
         def _():
@@ -310,13 +313,20 @@
             fwd_d2(t - 1).start()
             compact(t - 1)
 
-        even = t % 2 == 0
-
-        @pl.when(t == NZ)
+        @pl.when(t == NZ - 1)
         def _():
             across(5)
             across(4)
+            relay(NZ - 1)
+
+        even = t % 2 == 0
+
+        @pl.when(t == NZ)
+        def _():
+            home(5)
+            home(4)
             across(3)
+            across(2)
 
         @pl.when((t > 0) & even)
         def _():
@@ -371,21 +381,20 @@
             send_grads(3)
 
             def rest(m, carry):
-                across((6 + m) * (m < 2) + (4 - m) * (m >= 2))
+                across((6 + m) * (m < 2) + (3 - m) * (m >= 2))
                 return carry
 
-            lax.fori_loop(0, 5, rest, 0)
-            home(5)
+            lax.fori_loop(0, 4, rest, 0)
+            home(3)
 
         @pl.when(j == 1)
         def _():
             reduce[3].start()
-            home(4)
+            home(2)
 
         @pl.when(j == 2)
         def _():
             reduce[2].start()
-            home(3)
 
         return carry
 
@@ -403,10 +412,10 @@
     reduce[5].start()
 
     def near_home(m, carry):
-        home(2 - m)
-        return carry
-
-    lax.fori_loop(0, 3, near_home, 0)
+        home(1 - m)
+        return carry
+
+    lax.fori_loop(0, 2, near_home, 0)
     accumulate(3, False)
     gg_ref[...] = acc[0].T.astype(BF)
     gu_ref[...] = acc[1].T.astype(BF)

time: 149 us -> 152 us (1.020)
  Pallas kernels: 141 us -> 145 us
    pallas_call x1, Pallas kernels: 141 us -> 145 us  [on_device(): pl.pallas_call(kernel, out_shape=(jax.ShapeDtypeStruct((T, D), BF), jax.S...]
where the time goes in v6:
time: 152 us; the launch traced here: 150 us
  Pallas kernels  145 us (95%)
  local copies, waits for them, and re-layouts  4.58 us (3%)
    pallas_call x1, Pallas kernels, on_device(): pl.pallas_call(kernel, out_shape=(jax.ShapeDtypeStruct((T, D), BF), jax.S...  145 us
    unnamed x10, local copies, waits for them, and re-layouts  4.58 us

profile of v6, /device:TPU:1, one launch (start us, length us, event | category | flops | bytes accessed | tf_op | source)
XLA Modules:
  0.0 149.8 jit_solution(14014293241814134874)
XLA Ops:
  0.6 144.5 %shard_map.102 = (bf16[128,3584]{1,0:T(8,128)(2,1)}, bf16[896,256]{1,0:T(8,128)(2,1)}, bf16[896,256]{1,0:T(8,128)(2,1)}, bf16[256,896]{1,0:T(8,128)(2,1)}) custom-call(bf16[128,3584]{1,0:T(8,128)(2,1)} %tok_hbm.1, bf16[128,3584]{1,0:T(8,128)(2,1)} %grad_hbm.1, f32[1,128]{1,0:T(1,128)} %bitcast.14, s32[1,128]{1,0:T(1,128)} %bitcast.15, ...), custom_call_target="tpu_custom_call" | custom-call | flops 19730006016 | bytes 10000000 | tf_op jit(solution)/shard_map/pallas_call | solution.py:491
  145.2 0.0 copy-start.2
  145.2 0.0 copy-start.1
  145.2 0.0 copy-start
  145.2 2.3 %copy.15 = bf16[128,3584]{1,0:T(8,128)(2,1)} copy(bf16[128,3584]{1,0:T(8,128)(2,1)} %get-tuple-element.16) | data formatting | bytes 1835008
  147.5 0.0 copy-done.2
  147.5 0.8 copy.16
  148.2 0.0 copy-done.1
  148.2 0.8 copy.17
  149.0 0.0 copy-done
  149.0 0.8 copy.18
Async XLA Ops:
  145.2 2.3 %copy-start.2 = (bf16[896,256]{1,0:T(8,128)(2,1)S(1)}, bf16[896,256]{1,0:T(8,128)(2,1)}, u32[]{:S(2)}) copy-start(bf16[896,256]{1,0:T(8,128)(2,1)} %get-tuple-element.9) | copy-start | bytes 1376260
  145.2 3.1 %copy-start.1 = (bf16[896,256]{1,0:T(8,128)(2,1)S(1)}, bf16[896,256]{1,0:T(8,128)(2,1)}, u32[]{:S(2)}) copy-start(bf16[896,256]{1,0:T(8,128)(2,1)} %get-tuple-element.10) | copy-start | bytes 1376260
  145.2 3.8 %copy-start = (bf16[256,896]{1,0:T(8,128)(2,1)S(1)}, bf16[256,896]{1,0:T(8,128)(2,1)}, u32[]{:S(2)}) copy-start(bf16[256,896]{1,0:T(8,128)(2,1)} %get-tuple-element.11) | copy-start | bytes 1376260

commit v7 on v5

--- a/solution.py
+++ b/solution.py
@@ -156,7 +156,7 @@
         send_unit(k, 1).start()
         return carry
 
-    lax.fori_loop(0, NZ, send_one, 0)
+    lax.fori_loop(0, 5, send_one, 0)
     for copy in local[2:]:
         copy.wait()
     back = jnp.where(known, number * UNIT + position, -1000.0)
@@ -302,6 +302,11 @@
                 send_unit(t, h).wait_recv()
                 fwd_y(t, h).start()
             fwd_d1(t).start()
+
+        @pl.when((t > 0) & (t < 4))
+        def _():
+            send_unit(t + 4, 0).start()
+            send_unit(t + 4, 1).start()
 
         @pl.when(t > 0)
         def _():

time: 149 us -> 149 us (level)
  the two profiles are of different devices: /device:TPU:1 before, /device:TPU:101 now
where the time goes in v7:
time: 149 us
  Pallas kernels  144 us (97%)
  local copies, waits for them, and re-layouts  4.58 us (3%)
    pallas_call x1, Pallas kernels, on_device(): pl.pallas_call(kernel, out_shape=(jax.ShapeDtypeStruct((T, D), BF), jax.S...  144 us
    unnamed x10, local copies, waits for them, and re-layouts  4.58 us

profile of v7, /device:TPU:101, one launch (start us, length us, event | category | flops | bytes accessed | tf_op | source)
XLA Modules:
  0.0 149.1 jit_solution(15963997947244738597)
XLA Ops:
  0.6 143.8 %shard_map.102 = (bf16[128,3584]{1,0:T(8,128)(2,1)}, bf16[896,256]{1,0:T(8,128)(2,1)}, bf16[896,256]{1,0:T(8,128)(2,1)}, bf16[256,896]{1,0:T(8,128)(2,1)}) custom-call(bf16[128,3584]{1,0:T(8,128)(2,1)} %tok_hbm.1, bf16[128,3584]{1,0:T(8,128)(2,1)} %grad_hbm.1, f32[1,128]{1,0:T(1,128)} %bitcast.14, s32[1,128]{1,0:T(1,128)} %bitcast.15, ...), custom_call_target="tpu_custom_call" | custom-call | flops 19730006016 | bytes 10000000 | tf_op jit(solution)/shard_map/pallas_call | solution.py:487
  144.5 0.0 copy-start.2
  144.5 0.0 copy-start.1
  144.5 0.0 copy-start
  144.5 2.3 %copy.15 = bf16[128,3584]{1,0:T(8,128)(2,1)} copy(bf16[128,3584]{1,0:T(8,128)(2,1)} %get-tuple-element.16) | data formatting | bytes 1835008
  146.8 0.0 copy-done.2
  146.8 0.8 copy.16
  147.5 0.0 copy-done.1
  147.5 0.8 copy.17
  148.3 0.0 copy-done
  148.3 0.8 copy.18
Async XLA Ops:
  144.5 2.3 %copy-start.2 = (bf16[896,256]{1,0:T(8,128)(2,1)S(1)}, bf16[896,256]{1,0:T(8,128)(2,1)}, u32[]{:S(2)}) copy-start(bf16[896,256]{1,0:T(8,128)(2,1)} %get-tuple-element.9) | copy-start | bytes 1376260
  144.5 3.1 %copy-start.1 = (bf16[896,256]{1,0:T(8,128)(2,1)S(1)}, bf16[896,256]{1,0:T(8,128)(2,1)}, u32[]{:S(2)}) copy-start(bf16[896,256]{1,0:T(8,128)(2,1)} %get-tuple-element.10) | copy-start | bytes 1376260
  144.5 3.8 %copy-start = (bf16[256,896]{1,0:T(8,128)(2,1)S(1)}, bf16[256,896]{1,0:T(8,128)(2,1)}, u32[]{:S(2)}) copy-start(bf16[256,896]{1,0:T(8,128)(2,1)} %get-tuple-element.11) | copy-start | bytes 1376260
